TPU v7x, 128 devices: a whole 4x4x4 slice. The times are simulated.
128 devices in a mesh: row: 8 (over y, core), col: 16 (over z, x).
Axes of the slice: x: 4, y: 4, z: 4, core: 2. Of those that a mesh axis runs over, the one named last changes fastest.
Arguments:
- jac_row: bfloat16 [8, 16, 16, 2, 64, 3, 576], P('row', 'col'), may hold values from -0.25 to 0.25
- jac_col: bfloat16 [8, 16, 16, 2, 64, 3, 576], P('row', 'col'), may hold values from -0.25 to 0.25
- point_inv: bfloat16 [8, 16, 16, 2, 64, 9], P('row', 'col'), as said below
- pair_counts: int32 [8, 16, 16, 2], P('row', 'col'), may hold values from 16 to 64, as said below
- camera_blocks: float32 [16, 576, 576], P('row'), as said below
- right_side: float32 [16, 576], P('row'), may hold values from -300 to 300
Outputs:
- pair_blocks: float32 [16, 16, 576, 576], P('row', 'col')
- diagonal_blocks: float32 [16, 576, 576], P('row')
- solution: float32 [16, 576], P('row')
- residual: float32 [16, 576], P('row')
Inputs may be any that keep to these rules, and one draw needn't show every extreme that they name: `pair_counts`: one co-visibility list of every device holds 64 live tracks. `point_inv`: each 3 x 3 block is symmetric positive definite. `camera_blocks`: each block is symmetric; S and its diagonal blocks are positive definite.
All inputs are finite; a program needn't handle non-finite values.
Results may differ from a plain program's by a relative error of at most 0.0049.
Values may be sent and summed in bfloat16 or wider, within the bound.
A program may use at most 256 MiB of HBM per device.

v0:
```python
import jax
import jax.numpy as jnp
from jax import lax
from jax.sharding import PartitionSpec as P

ITERS = 2


def apply_inverse(inverse, jac):
    inv = inverse.astype(jnp.float32)
    wide = jac.astype(jnp.float32)
    rows = [
        inv[..., 3 * k, None] * wide[..., 0, :]
        + inv[..., 3 * k + 1, None] * wide[..., 1, :]
        + inv[..., 3 * k + 2, None] * wide[..., 2, :]
        for k in range(3)
    ]
    return jnp.stack(rows, axis=-2).astype(jnp.bfloat16)


def solve_blocks(factor, vec):
    half = lax.linalg.triangular_solve(factor, vec[..., None], left_side=True, lower=True)
    whole = lax.linalg.triangular_solve(factor, half, left_side=True, lower=True, transpose_a=True)
    return whole[..., 0]


def form_pairs(pieces):
    w_row, w_col, inverse = pieces
    col_img = apply_inverse(inverse, w_col)
    tile = jnp.einsum("jamkp,jamkq->ajpq", w_row, col_img, preferred_element_type=jnp.float32)
    own_col = jnp.einsum("jamkp,jamkq->ajpq", w_col, col_img, preferred_element_type=jnp.float32)
    return (tile, own_col)


def form_all(pieces):
    w_row, w_col, inverse = pieces
    tile, own_col = form_pairs(pieces)
    row_img = apply_inverse(inverse, w_row)
    own_row = jnp.einsum("jamkp,jamkq->apq", w_row, row_img, preferred_element_type=jnp.float32)
    return (tile, own_col, own_row)


def body(jac_row, jac_col, point_inv, pair_counts, camera_blocks, right_side):
    groups = jac_row.shape[2]
    rows_per = jac_row.shape[3]
    slots = jac_row.shape[4]
    w_row = jac_row.reshape(jac_row.shape[2:])
    w_col = jac_col.reshape(jac_col.shape[2:])
    inverse = point_inv.reshape(point_inv.shape[2:])
    counts = pair_counts.reshape(pair_counts.shape[2:])
    live = lax.broadcasted_iota(jnp.int32, (groups, rows_per, slots), 2) < counts[:, :, None]
    masked = inverse * live[..., None].astype(jnp.bfloat16)
    formed = form_all(
        (
            lax.all_to_all(w_row, "col", split_axis=0, concat_axis=2, tiled=True),
            lax.all_to_all(w_col, "col", split_axis=0, concat_axis=2, tiled=True),
            lax.all_to_all(masked, "col", split_axis=0, concat_axis=2, tiled=True),
        )
    )
    tile, own_col, row_terms = formed
    cols_per = tile.shape[1]
    col_terms = lax.psum(jnp.sum(own_col, axis=0), "row")
    row_here = lax.axis_index("row")
    col_here = lax.axis_index("col")
    slot_here = col_here * cols_per - row_here * rows_per
    select = (jnp.arange(rows_per, dtype=jnp.int32) == slot_here).astype(jnp.float32)
    safe = jnp.clip(slot_here, 0, rows_per - 1)
    self_pair = lax.dynamic_index_in_dim(tile[:, 0], safe, 0, keepdims=False)
    mirrored = self_pair + self_pair.T
    own_terms = row_terms + select[:, None, None] * col_terms[0][None]
    pair_terms = select[:, None, None] * mirrored[None]
    own_sum, pair_sum = lax.psum((own_terms, pair_terms), "col")
    diagonal = camera_blocks - own_sum
    factor = jnp.linalg.cholesky(diagonal - pair_sum)
    high = lax.Precision.HIGHEST
    solution = jnp.zeros_like(right_side)
    residual = right_side

    def norm_of(first, second):
        return lax.psum(jnp.sum(first * second), "row")

    pre_res = solve_blocks(factor, residual)
    direction = pre_res
    rz_now = norm_of(residual, pre_res)
    for step in range(ITERS):
        gathered = lax.all_gather(direction, "row", axis=0, tiled=True)
        column_vec = lax.dynamic_slice_in_dim(gathered, col_here * cols_per, cols_per, 0)
        forward = jnp.einsum("ajpq,jq->ap", tile, column_vec, precision=high)
        backward = jnp.einsum("ajpq,ap->jq", tile, direction, precision=high)
        own = jnp.einsum("apq,aq->ap", diagonal, direction, precision=high)
        zeros = jnp.zeros(gathered.shape, jnp.float32)
        spread = lax.dynamic_update_slice_in_dim(zeros, forward, row_here * rows_per, 0)
        spread = spread + lax.dynamic_update_slice_in_dim(zeros, backward, col_here * cols_per, 0)
        summed = lax.psum(spread, ("row", "col"))
        image = own - lax.dynamic_slice_in_dim(summed, row_here * rows_per, rows_per, 0)
        alpha = rz_now / lax.psum(jnp.sum(direction * image), "row")
        solution = solution + alpha * direction
        residual = residual - alpha * image
        if step + 1 < ITERS:
            pre_res = solve_blocks(factor, residual)
            rz_next = norm_of(residual, pre_res)
            direction = pre_res + rz_next / rz_now * direction
            rz_now = rz_next
    return (tile, diagonal, solution, residual)


def solution(mesh):
    return jax.shard_map(
        body,
        mesh=mesh,
        in_specs=(
            P("row", "col", None, None, None, None, None),
            P("row", "col", None, None, None, None, None),
            P("row", "col", None, None, None, None),
            P("row", "col", None, None),
            P("row", None, None),
            P("row", None),
        ),
        out_specs=(
            P("row", "col", None, None),
            P("row", None, None),
            P("row", None),
            P("row", None),
        ),
        check_vma=False,
    )
```

profile of v0, /device:TPU:0, one launch (start us, length us, event | category | flops | bytes accessed | tf_op | source)
XLA Modules:
  0.0 1162.7 jit_solution(10405863025008993494)
XLA Ops:
  9.1 15.4 %all_to_all.39 = bf16[16,2,576]{2,1,0:T(2,128)(2,1)S(1)} all-to-all(bf16[16,2,576]{2,1,0:T(2,128)(2,1)S(1)} %reshape.720), channel_id=1, replica_groups=mesh['row'=8,'col'=16] {'col'}, dimensions={0} | all-to-all | bytes 73728 | tf_op jit(solution)/shard_map/all_to_all | solution.py:57
  24.4 95.2 %all_to_all.40 = bf16[16,2,64,3,576]{4,2,3,1,0:T(8,128)(2,1)} all-to-all(bf16[16,2,64,3,576]{4,2,3,1,0:T(8,128)(2,1)} %bitcast.484), channel_id=1, replica_groups=mesh['row'=8,'col'=16] {'col'}, dimensions={0} | all-to-all | bytes 14155776 | tf_op jit(solution)/shard_map/all_to_all | solution.py:56
  135.9 12.9 %copy.116 = f32[1,2,16,64,3,576]{5,3,2,4,1,0:T(8,128)} copy(f32[1,2,16,64,3,576]{5,3,4,1,2,0:T(8,128)} %bitcast_convert_fusion) | data formatting | bytes 28311552 | tf_op jit(solution)/shard_map/convert_element_type | solution.py:11
  177.9 59.9 %all-to-all-done.2 = bf16[16,2,64,3,576]{4,2,3,1,0:T(8,128)(2,1)} async-done(((bf16[16,2,64,3,576]{4,2,3,1,0:T(8,128)(2,1)}), bf16[16,2,64,3,576]{4,2,3,1,0:T(8,128)(2,1)}, u32[]{:S(2)}, u32[]{:S(2)}) %all-to-all-start.2) | async-done | bytes 7077920 | tf_op jit(solution)/shard_map/all_to_all | solution.py:55
  248.8 12.9 %copy.124 = f32[1,2,16,64,3,576]{5,3,2,4,1,0:T(8,128)} copy(f32[1,2,16,64,3,576]{5,3,4,1,2,0:T(8,128)} %bitcast_convert_fusion.1) | data formatting | bytes 28311552 | tf_op jit(solution)/shard_map/convert_element_type | solution.py:11
  305.2 16.8 %fusion.19 = (bf16[2,1024,1,576]{1,3,2,0:T(8,128)(2,1)}, bf16[2,1024,1,576]{1,3,2,0:T(8,128)(2,1)}, bf16[2,1024,1,576]{1,3,2,0:T(8,128)(2,1)}, bf16[2,1024,1,576...) fusion(f32[1,2,1024,1,576]{2,4,1,3,0:T(8,128)} %copy.246, ...), kind=kLoop, calls=%fused_computation.31 | loop fusion | flops 42467328 | bytes 42541056 | tf_op jit(solution)/shard_map/stack | solution.py:18
  344.7 55.7 %all-reduce.10.cloned.1.call-done = f32[576,576]{0,1:T(8,128)} async-done(((f32[576,576]{0,1:T(8,128)}), f32[576,576]{0,1:T(8,128)}) %all-reduce.10.cloned.1.call-update) | async-done | bytes 1327120 | tf_op jit(solution)/shard_map/psum | solution.py:62
  421.7 110.0 %all-reduce.12.cloned.1.call-done = (f32[2,576,576]{1,2,0:T(8,128)}, f32[2,576,576]{1,2,0:T(8,128)}) async-done(((f32[2,576,576]{1,2,0:T(8,128)}, f32[2,576,576]{1,2,0:T(8,128)}), (f32[2,576,576]{1,2,0:T(8,128)}, f32[2,576,576]{1,2,0:T(8,128)})) %all-reduce.12.cloned.1.call-update) | async-done | bytes 5308432 | tf_op jit(solution)/shard_map/psum | solution.py:72
  546.4 23.5 %custom-call.46 = f32[2,128,128]{2,1,0:T(8,128)S(1)} custom-call(f32[2,128,128]{2,1,0:T(8,128)S(1)} %cholesky.357), custom_call_target="Cholesky" | custom-call | tf_op jit(solution)/shard_map/jit(cholesky)/cholesky | solution.py:74
  571.7 19.7 %custom-call.47 = f32[2,1,128,128]{2,3,1,0:T(8,128)S(1)} custom-call(f32[2,1,128,128]{3,2,1,0:T(8,128)S(1)} %select_bitcast_fusion.3), custom_call_target="InvertDiagBlocksLowerTriangular" | custom-call | tf_op jit(solution)/shard_map/jit(cholesky)/cholesky | solution.py:74
  595.9 25.3 %custom-call.48 = f32[2,128,128]{2,1,0:T(8,128)} custom-call(f32[2,128,128]{2,1,0:T(8,128)} %cholesky.361), custom_call_target="Cholesky" | custom-call | tf_op jit(solution)/shard_map/jit(cholesky)/cholesky | solution.py:74
  622.8 21.1 %custom-call.49 = f32[2,1,128,128]{2,3,1,0:T(8,128)} custom-call(f32[2,1,128,128]{3,2,1,0:T(8,128)} %get-tuple-element.92), custom_call_target="InvertDiagBlocksLowerTriangular" | custom-call | tf_op jit(solution)/shard_map/jit(cholesky)/cholesky | solution.py:74
  649.3 24.9 %custom-call.50 = f32[2,128,128]{2,1,0:T(8,128)} custom-call(f32[2,128,128]{2,1,0:T(8,128)} %cholesky.366), custom_call_target="Cholesky" | custom-call | tf_op jit(solution)/shard_map/jit(cholesky)/cholesky | solution.py:74
  675.9 21.2 %custom-call.51 = f32[2,1,128,128]{2,3,1,0:T(8,128)} custom-call(f32[2,1,128,128]{3,2,1,0:T(8,128)} %get-tuple-element.90), custom_call_target="InvertDiagBlocksLowerTriangular" | custom-call | tf_op jit(solution)/shard_map/jit(cholesky)/cholesky | solution.py:74
  702.5 24.9 %custom-call.52 = f32[2,128,128]{2,1,0:T(8,128)} custom-call(f32[2,128,128]{2,1,0:T(8,128)} %cholesky.371), custom_call_target="Cholesky" | custom-call | tf_op jit(solution)/shard_map/jit(cholesky)/cholesky | solution.py:74
  729.8 20.5 %custom-call.53 = f32[2,1,128,128]{2,3,1,0:T(8,128)S(1)} custom-call(f32[2,1,128,128]{3,2,1,0:T(8,128)} %get-tuple-element.88), custom_call_target="InvertDiagBlocksLowerTriangular" | custom-call | tf_op jit(solution)/shard_map/jit(cholesky)/cholesky | solution.py:74
  772.2 14.5 %while.8 = (s32[]{:T(128)}, f32[2,576,576]{2,1,0:T(8,128)}, s32[4,2]{0,1:T(2,128)S(1)}, f32[4,2,128,128]{3,2,0,1:T(8,128)}, s32[]{:T(128)}) while((s32[]{:T(128)}, f32[2,576,576]{2,1,0:T(8,128)}, s32[4,2]{0,1:T(2,128)S(1)}, f32[4,2,128,128]{3,2,0,1:T(8,128)}, s32[]{:T(128)}) %tuple.80), condition=%wide.while_cond.1, body=%wide.while_body.1.sunk | while | flops 2 | bytes 263777 | solution.py:23
  788.8 99.9 %custom-call.58 = f32[2,5,128,128]{2,3,1,0:T(8,128)} custom-call(f32[2,5,128,128]{3,2,1,0:T(8,128)} %pad_maximum_fusion.1), custom_call_target="InvertDiagBlocksLowerTriangular" | custom-call | tf_op jit(solution)/shard_map/triangular_solve/custom-call.10 | solution.py:23
  912.5 13.2 %all-gather = f32[16,576,1]{1,2,0:T(1,128)S(1)} all-gather(f32[2,576,1]{1,2,0:T(1,128)S(1)} %copy.197), channel_id=2, replica_groups=mesh['row'=8,'col'=16] {'row'}, dimensions={0}, use_global_device_ids=true | all-gather | bytes 41472 | tf_op jit(solution)/shard_map/all_gather | solution.py:86
  929.9 65.1 %psum.67 = f32[16,576]{1,0:T(8,128)S(1)} all-reduce(f32[16,576]{1,0:T(8,128)S(1)} %add.199), channel_id=1, replica_groups=mesh['row'=8,'col'=16] {'row','col'}, use_global_device_ids=true, to_apply=%region_15.18 | all-reduce | flops 9216 | bytes 73728 | tf_op jit(solution)/shard_map/psum | solution.py:94
  995.6 14.8 %all-reduce.6 = (f32[]{:T(128)}, f32[]{:T(128)}) all-reduce(f32[]{:T(128)} %get-tuple-element.59, f32[]{:T(128)} %get-tuple-element.58), channel_id=1, replica_groups=mesh['row'=8,'col'=16] {'row'}, use_global_device_ids=true, to_apply=%region_14.17 | all-reduce | flops 2 | bytes 16 | tf_op jit(solution)/shard_map/psum | solution.py:80
  1034.4 13.0 %psum.69 = f32[]{:T(128)} all-reduce(f32[]{:T(128)} %fusion.112), channel_id=1, replica_groups=mesh['row'=8,'col'=16] {'row'}, use_global_device_ids=true, to_apply=%region_19.22 | all-reduce | flops 1 | bytes 8 | tf_op jit(solution)/shard_map/psum | solution.py:80
  1069.5 63.0 %psum.70 = f32[16,576]{1,0:T(8,128)S(1)} all-reduce(f32[16,576]{1,0:T(8,128)S(1)} %add.203), channel_id=1, replica_groups=mesh['row'=8,'col'=16] {'row','col'}, use_global_device_ids=true, to_apply=%region_20.23 | all-reduce | flops 9216 | bytes 73728 | tf_op jit(solution)/shard_map/psum | solution.py:94
  1135.3 14.1 %psum.71 = f32[]{:T(128)} all-reduce(f32[]{:T(128)} %multiply_reduce_fusion), channel_id=1, replica_groups=mesh['row'=8,'col'=16] {'row'}, use_global_device_ids=true, to_apply=%region_22.25 | all-reduce | flops 1 | bytes 8 | tf_op jit(solution)/shard_map/psum | solution.py:96
  (228 shorter events, 300.7 us)
Async XLA Ops:
  119.7 118.1 %all-to-all-start.2 = ((bf16[16,2,64,3,576]{4,2,3,1,0:T(8,128)(2,1)}), bf16[16,2,64,3,576]{4,2,3,1,0:T(8,128)(2,1)}, u32[]{:S(2)}, u32[]{:S(2)}) async-start(bf16[16,2,64,3,576]{4,2,3,1,0:T(8,128)(2,1)} %bitcast.485), calls=%async_computation.2 | async-start | bytes 15728640 | tf_op jit(solution)/shard_map/all_to_all | solution.py:55
  124.4 276.0 %all-reduce.10.cloned.1.call-start = ((), (), s32[]{:S(2)}) async-start(), calls=%async_computation.3 | async-start | bytes 2949120 | tf_op jit(solution)/shard_map/psum | solution.py:62
  297.7 7.5 slice-start
  297.7 7.5 slice-start.1
  305.2 16.8 %copy-start.2 = (bf16[1,2,16,64,3,576]{5,3,2,4,1,0:T(8,128)(2,1)S(1)}, bf16[1,2,16,64,3,576]{5,3,2,4,1,0:T(8,128)(2,1)}, u32[]{:S(2)}) copy-start(bf16[1,2,16,64,3,576]{5,3,2,4,1,0:T(8,128)(2,1)} %copy.122) | copy-start | bytes 21233668
  305.2 25.0 %slice-start.2 = ((s8[7864320]{0:T(1024)(128)(4,1)}), s8[4194304]{0:T(1024)(128)(4,1)S(1)}, s32[]{:S(2)}) async-start(s8[7864320]{0:T(1024)(128)(4,1)} %bitcast.488), calls=%async_computation.7 | async-start | bytes 8388608
  322.0 8.2 slice-start.3
  322.1 8.2 copy-start.4
  322.1 8.2 copy-start.5
  322.1 8.2 copy-start.6
  337.1 194.6 %all-reduce.12.cloned.1.call-start = ((), (), s32[]{:S(2)}) async-start(), calls=%async_computation.4 | async-start | bytes 11796480 | tf_op jit(solution)/shard_map/psum | solution.py:72
  544.8 1.6 copy-start.3
  646.0 81.4 %copy-start.11 = (pred[128,128]{1,0:T(8,128)(4,1)S(1)}, pred[128,128]{1,0:T(8,128)(4,1)}, u32[]{:S(2)}) copy-start(pred[128,128]{1,0:T(8,128)(4,1)} %iota_compare_fusion.3) | copy-start | bytes 49156
  646.0 122.3 %copy-start.7 = (pred[576,576]{1,0:T(8,128)(4,1)S(1)}, pred[576,576]{1,0:T(8,128)(4,1)}, u32[]{:S(2)}) copy-start(pred[576,576]{1,0:T(8,128)(4,1)} %iota_compare_fusion) | copy-start | bytes 995332
  648.0 0.7 copy-start.8
  701.2 0.7 copy-start.9
  768.3 2.4 copy-start.14
  768.3 18.4 %copy-start.10 = (f32[128,64]{1,0:T(8,128)S(1)}, f32[128,64]{1,0:T(8,128)}, u32[]{:S(2)}) copy-start(f32[128,64]{1,0:T(8,128)} %pad_convert_fusion) | copy-start | bytes 98308
  770.6 1.6 copy-start.1
  770.7 118.0 %copy-start.13 = (f32[2,128,1]{1,0,2:T(2,128)S(1)}, f32[2,128,1]{1,0,2:T(2,128)}, u32[]{:S(2)}) copy-start(f32[2,128,1]{1,0,2:T(2,128)} %slice.413) | copy-start | bytes 3076
  770.7 120.5 %copy-start.12 = (f32[2,576]{1,0:T(2,128)S(1)}, f32[2,576]{1,0:T(2,128)}, u32[]{:S(2)}) copy-start(f32[2,576]{1,0:T(2,128)} %param.15) | copy-start | bytes 13828
  888.7 22.2 %copy-start = (f32[2,576,576]{1,2,0:T(8,128)S(1)}, f32[2,576,576]{1,2,0:T(8,128)}, u32[]{:S(2)}) copy-start(f32[2,576,576]{1,2,0:T(8,128)} %get-tuple-element.73) | copy-start | bytes 7962628
Sparse Core Ops, SparseCore 0:
  337.2 63.1 all-reduce.9
  413.5 118.1 all-reduce.11
where the time goes:
time: 1170 us; the launch traced here: 1160 us
  other arithmetic  365 us (31%)
  blocking collectives  307 us (26%)
  waiting for transfers between devices  226 us (19%)
  local copies, waits for them, and re-layouts  141 us (12%)
  matrix products  100 us (9%)
  between operations  19.1 us (2%)
    another operation x21, other arithmetic, body(): factor = jnp.linalg.cholesky(diagonal - pair_sum)  203 us
    psum x2, blocking collectives, body(): summed = lax.psum(spread, ('row', 'col'))  128 us
    psum x1, waiting for transfers between devices, body(): own_sum, pair_sum = lax.psum((own_terms, pair_terms), 'col')  110 us
    another operation x23, other arithmetic, solve_blocks(): lax.linalg.triangular_solve(factor, half, left_side=True, lower=True, tra...  106 us
    all_to_all x1, blocking collectives, body(): lax.all_to_all(w_col, 'col', split_axis=0, concat_axis=2, tiled=True)  95.2 us
    all_to_all x1, waiting for transfers between devices, body(): lax.all_to_all(w_row, 'col', split_axis=0, concat_axis=2, tiled=True)  59.9 us
    psum x1, waiting for transfers between devices, body(): col_terms = lax.psum(jnp.sum(own_col, axis=0), 'row')  55.7 us
    unnamed x58, local copies, waits for them, and re-layouts  49.5 us
  transfers between devices with their start and end apart: 3, of which 3 were waited for; matrix products, arithmetic and copies ran while one was open for 6% of the time, Pallas kernels for 0%

commit v1 on v0

v1 whole, which is shorter than its diff:
```python
import functools
import jax
import jax.numpy as jnp
from jax import lax
from jax.experimental import pallas as pl
from jax.experimental.pallas import tpu as pltpu
from jax.sharding import PartitionSpec as P

MESH = pl.DeviceIdType.MESH
F32 = jnp.float32
BF16 = jnp.bfloat16
NROW, NCOL, GR, SLOT, BLK = 8, 16, 2, 64, 576
K3 = 3 * SLOT
CH = 72
ITERS = 2


def tn(lhs, rhs):
    return lax.dot_general(lhs, rhs, (((0,), (0,)), ((), ())), preferred_element_type=F32)


def form_kernel(minv, wrow, wcol, cam, tile, dchunk, pg_out,
                rmin, rrow, rcol, ownr, ownc, big, srow, qrow, scol, qcol, pg, camv,
                send_sem, recv_sem, loc_sem, rs_send, rs_recv, cs_send, cs_recv, pg_send, pg_recv):
    r = lax.axis_index("row")
    c = lax.axis_index("col")
    cg = c // GR
    half = c // NROW
    g = GR * r + half
    part = c % NROW

    def col_dst(i):
        return cg, (c % GR) * NROW + i

    barrier = pltpu.get_barrier_semaphore()

    def greet_row(d, n):
        pl.semaphore_signal(barrier, inc=1, device_id=(r, lax.rem(c + d, NCOL)), device_id_type=MESH)
        return n
    lax.fori_loop(1, NCOL, greet_row, 0)

    def greet_col(i, n):
        other = jnp.logical_or(i != r, g != c)

        @pl.when(other)
        def _():
            pl.semaphore_signal(barrier, inc=1, device_id=(i, g), device_id_type=MESH)
        return n
    lax.fori_loop(0, NROW, greet_col, 0)
    own_dst = jnp.logical_and(r == cg, c // NROW == c % GR)
    pl.semaphore_wait(barrier, NCOL - 1 + NROW - own_dst.astype(jnp.int32))

    def copies(d):
        j = lax.rem(c + d, NCOL)
        dev = (r, j)
        return [pltpu.make_async_remote_copy(src_ref=src.at[j], dst_ref=dst.at[d], send_sem=send_sem.at[n, d],
                                             recv_sem=recv_sem.at[n, d], device_id=dev, device_id_type=MESH)
                for n, (src, dst) in enumerate(((minv, rmin), (wcol, rcol), (wrow, rrow)))]

    def locals_():
        return [pltpu.make_async_copy(src.at[c], dst.at[0], loc_sem.at[n])
                for n, (src, dst) in enumerate(((minv, rmin), (wcol, rcol), (wrow, rrow)))] + [
            pltpu.make_async_copy(cam.at[c], camv, loc_sem.at[3])]

    for cp in locals_():
        cp.start()

    def start(d, n):
        for cp in copies(d):
            cp.start()
        return n
    lax.fori_loop(1, NCOL, start, 0)

    tile[...] = jnp.zeros_like(tile)
    ownr[...] = jnp.zeros_like(ownr)
    ownc[...] = jnp.zeros_like(ownc)

    row_i = lax.broadcasted_iota(jnp.int32, (SLOT, K3), 0)
    col_i = lax.broadcasted_iota(jnp.int32, (SLOT, K3), 1)
    eye = jnp.where(lax.rem(col_i, SLOT) == row_i, 1.0, 0.0).astype(F32)

    def chunk(d):
        for a in range(GR):
            ent = rmin[d, 8 * a:8 * a + 8, :].astype(F32)
            for k in range(3):
                big[SLOT * k:SLOT * (k + 1), :] = (eye * ent[k:k + 1, :]).astype(BF16)
            wr = rrow[d, K3 * a:K3 * (a + 1), :]
            wc = rcol[d, K3 * a:K3 * (a + 1), :]
            ci = jnp.dot(big[...], wc, preferred_element_type=F32).astype(BF16)
            ri = jnp.dot(big[...], wr, preferred_element_type=F32).astype(BF16)
            for lo, hi in ((0, 256), (256, 512), (512, 576)):
                tile[a, lo:hi, :] += tn(wr[:, lo:hi], ci)
                ownr[a, lo:hi, :] += tn(wr[:, lo:hi], ri)
                ownc[lo:hi, :] += tn(wc[:, lo:hi], ci)

    for cp in locals_()[:3]:
        cp.wait()
    chunk(0)

    def step(d, n):
        for cp in copies(d):
            cp.wait_recv()
        chunk(d)
        return n
    lax.fori_loop(1, NCOL, step, 0)

    for m in range(NCOL):
        a, i = divmod(m, NROW)
        srow[m] = ownr[a, CH * i:CH * (i + 1), :].astype(BF16)
    for i in range(NROW):
        scol[i] = ownc[CH * i:CH * (i + 1), :].astype(BF16)

    def row_copy(d):
        j = lax.rem(c + d, NCOL)
        return pltpu.make_async_remote_copy(src_ref=srow.at[j], dst_ref=qrow.at[d], send_sem=rs_send.at[d],
                                            recv_sem=rs_recv.at[d], device_id=(r, j), device_id_type=MESH)

    def col_copy(i):
        return pltpu.make_async_remote_copy(src_ref=scol.at[i], dst_ref=qcol.at[r], send_sem=cs_send.at[i],
                                            recv_sem=cs_recv.at[r], device_id=col_dst(i), device_id_type=MESH)

    def stays(i):
        return jnp.logical_and(own_dst, i == part)

    def col_start(i, n):
        @pl.when(jnp.logical_not(stays(i)))
        def _():
            col_copy(i).start()

        @pl.when(stays(i))
        def _():
            qcol[r] = scol[i]
        return n
    lax.fori_loop(0, NROW, col_start, 0)

    def row_start(d, n):
        row_copy(d).start()
        return n
    lax.fori_loop(1, NCOL, row_start, 0)

    locals_()[3].wait()
    dchunk[...] = camv[...] - srow[c].astype(F32)

    def col_sum(i, n):
        @pl.when(jnp.logical_or(i != r, g != c))
        def _():
            pltpu.make_async_remote_copy(src_ref=scol.at[i], dst_ref=qcol.at[i], send_sem=cs_send.at[i],
                                         recv_sem=cs_recv.at[i], device_id=(i, g), device_id_type=MESH).wait_recv()
        dchunk[...] -= qcol[i].astype(F32)
        return n
    lax.fori_loop(0, NROW, col_sum, 0)

    def row_sum(d, n):
        row_copy(d).wait_recv()
        dchunk[...] -= qrow[d].astype(F32)
        return n
    lax.fori_loop(1, NCOL, row_sum, 0)

    is_p = cg == r

    def pg_copy(i):
        return pltpu.make_async_remote_copy(src_ref=dchunk, dst_ref=pg.at[i], send_sem=pg_send, recv_sem=pg_recv.at[i],
                                            device_id=(r, g), device_id_type=MESH)

    @pl.when(g != c)
    def _():
        pg_copy(part).start()

    def drain(d, n):
        for cp in copies(d):
            cp.wait_send()
        row_copy(d).wait_send()
        return n
    lax.fori_loop(1, NCOL, drain, 0)

    def drain_col(i, n):
        @pl.when(jnp.logical_not(stays(i)))
        def _():
            col_copy(i).wait_send()
        return n
    lax.fori_loop(0, NROW, drain_col, 0)

    @pl.when(g != c)
    def _():
        pg_copy(part).wait_send()

    def gather(i, n):
        src_c = (c % GR) * NROW + i

        @pl.when(jnp.logical_and(is_p, src_c != c))
        def _():
            pg_copy(i).wait_recv()
            pg_out[i] = pg[i]

        @pl.when(jnp.logical_and(is_p, src_c == c))
        def _():
            pg_out[i] = dchunk[...]

        @pl.when(jnp.logical_not(is_p))
        def _():
            rows = lax.broadcasted_iota(jnp.int32, (CH, BLK), 0) + i * CH
            cols = lax.broadcasted_iota(jnp.int32, (CH, BLK), 1)
            pg_out[i] = jnp.where(rows == cols, 1.0, 0.0).astype(F32)
        return n
    lax.fori_loop(0, NROW, gather, 0)


def form(minv, wrow, wcol, cam):
    any_ = pl.BlockSpec(memory_space=pl.ANY)
    vm = pl.BlockSpec(memory_space=pltpu.VMEM)
    dma = pltpu.SemaphoreType.DMA
    return pl.pallas_call(
        form_kernel,
        out_shape=(jax.ShapeDtypeStruct((GR, BLK, BLK), F32), jax.ShapeDtypeStruct((CH, BLK), F32),
                   jax.ShapeDtypeStruct((NROW, CH, BLK), F32)),
        in_specs=[any_] * 4,
        out_specs=(vm, vm, vm),
        scratch_shapes=[
            pltpu.VMEM((NCOL, 16, K3), BF16),
            pltpu.VMEM((NCOL, GR * K3, BLK), BF16),
            pltpu.VMEM((NCOL, GR * K3, BLK), BF16),
            pltpu.VMEM((GR, BLK, BLK), F32),
            pltpu.VMEM((BLK, BLK), F32),
            pltpu.VMEM((K3, K3), BF16),
            pltpu.VMEM((NCOL, CH, BLK), BF16),
            pltpu.VMEM((NCOL, CH, BLK), BF16),
            pltpu.VMEM((NROW, CH, BLK), BF16),
            pltpu.VMEM((NROW, CH, BLK), BF16),
            pltpu.VMEM((NROW, CH, BLK), F32),
            pltpu.VMEM((CH, BLK), F32),
            dma((3, NCOL)), dma((3, NCOL)), dma((4,)),
            dma((NCOL,)), dma((NCOL,)), dma((NROW,)), dma((NROW,)),
            dma, dma((NROW,)),
        ],
        compiler_params=pltpu.CompilerParams(collective_id=0, has_side_effects=True, vmem_limit_bytes=56 * 2**20),
        name="form",
    )(minv, wrow, wcol, cam)


def minv_table(point_inv, pair_counts):
    inv = point_inv.reshape(NCOL, GR, SLOT, 3, 3)
    live = lax.broadcasted_iota(jnp.int32, (NCOL, GR, SLOT), 2) < pair_counts.reshape(NCOL, GR)[:, :, None]
    masked = inv * live[..., None, None].astype(BF16)
    rows = jnp.transpose(masked, (0, 1, 3, 4, 2)).reshape(NCOL, GR, 3, K3)
    return jnp.pad(rows, ((0, 0), (0, 0), (0, 5), (0, 0))).reshape(NCOL, 16, K3)


def stack_rows(jac):
    return jnp.transpose(jac.reshape(jac.shape[2:]), (0, 1, 3, 2, 4)).reshape(NCOL, GR * K3, BLK)


def mm(lhs, rhs):
    return jnp.dot(lhs.astype(BF16), rhs.astype(BF16), preferred_element_type=F32)


def mm_high(lhs, rhs):
    return jnp.dot(lhs, rhs, preferred_element_type=F32, precision=lax.Precision.HIGHEST)


def inverse_kernel(pg, tile, xinv, pmat, pair, e, y, res, sem):
    r = lax.axis_index("row")
    c = lax.axis_index("col")
    is_p = (c // GR == r).astype(F32)
    cp = pltpu.make_async_copy(tile.at[c % GR], pair, sem)
    cp.start()
    rows = lax.broadcasted_iota(jnp.int32, (BLK, BLK), 0)
    cols = lax.broadcasted_iota(jnp.int32, (BLK, BLK), 1)
    eye = jnp.where(rows == cols, 1.0, 0.0).astype(F32)
    cp.wait()
    own = pair[...] * is_p
    p = pg[...] - own - own.T
    pmat[...] = p
    dd = p * eye
    s_row = lax.rsqrt(jnp.sum(dd, axis=0, keepdims=True))
    s_col = lax.rsqrt(jnp.sum(dd, axis=1, keepdims=True))
    b = p * s_row * s_col
    e[...] = eye - b
    e2 = mm(e[...], e[...])
    f2 = jnp.sum(e2 * e2)

    @pl.when(f2 < 0.9)
    def _():
        y[...] = e[...] + e2 + mm(e[...], e2)

    @pl.when(jnp.logical_not(f2 < 0.9))
    def _():
        big = jnp.max(jnp.sum(jnp.abs(eye - e[...]), axis=1, keepdims=True))
        y[...] = eye * (1.0 / big - 1.0)

    def residual(mul):
        out = e[...] - y[...] + mul(y[...], e[...])
        res[...] = out
        return jnp.sum(out * out)

    def more(state):
        step, size = state
        return jnp.logical_and(size > 1.6e-5, step < 64)

    def newton(state):
        step, _ = state

        def low():
            y[...] = y[...] + res[...] + mm(res[...], y[...])
            return residual(mm)

        def high():
            y[...] = y[...] + res[...] + mm_high(res[...], y[...])
            return residual(mm_high)
        return step + 1, lax.cond(step < 6, low, high)
    lax.while_loop(more, newton, (jnp.int32(0), residual(mm)))
    xinv[...] = (eye + y[...]) * s_row * s_col


def inverse(pg, tile):
    vm = pl.BlockSpec(memory_space=pltpu.VMEM)
    sq = jax.ShapeDtypeStruct((BLK, BLK), F32)
    return pl.pallas_call(
        inverse_kernel,
        out_shape=(sq, sq),
        in_specs=[vm, pl.BlockSpec(memory_space=pl.ANY)],
        out_specs=(vm, vm),
        scratch_shapes=[pltpu.VMEM((BLK, BLK), F32)] * 4 + [pltpu.SemaphoreType.DMA],
        compiler_params=pltpu.CompilerParams(vmem_limit_bytes=48 * 2**20),
        name="inverse",
    )(pg, tile)


LT = 5
REFINE = 2


def lanes(t):
    return 128 * t, min(128 * (t + 1), BLK)


def spread(mat, vec):
    rows = mat.shape[0]
    acc = jnp.zeros((rows, 128), F32)
    for t in range(LT):
        lo, hi = lanes(t)
        part = mat[:, lo:hi] * vec[t:t + 1, :hi - lo]
        if hi - lo < 128:
            part = jnp.concatenate([part, jnp.zeros((rows, 128 - (hi - lo)), F32)], axis=1)
        acc = acc + part
    return acc


def fold(acc):
    out = []
    for t in range(LT):
        lo, hi = lanes(t)
        blk = acc[lo:hi, :]
        if hi - lo < 128:
            blk = jnp.concatenate([blk, jnp.zeros((128 - (hi - lo), 128), F32)], axis=0)
        out.append(jnp.sum(blk.T, axis=0, keepdims=True))
    return jnp.concatenate(out + [jnp.zeros((8 - LT, 128), F32)], axis=0)


def columns(vec):
    return jnp.concatenate([jnp.broadcast_to(vec[t:t + 1, :], (128, 128)).T for t in range(LT)], axis=0)


def matvec(mat, vec):
    return fold(spread(mat, vec))


def cg_kernel(tile, dchunk, xinv, pmat, rhs, diag, sol, resid,
              zbuf, zsrc, cbuf, csrc, bbuf, bsrc, sbuf, ssrc, fbuf, fsrc, acc, state,
              g_loc, g_send, g_recv, zr_send, zc_send, z_recv, c_send, b_send, c_recv, b_recv,
              s_send, s_recv, f_send, f_recv):
    r = lax.axis_index("row")
    c = lax.axis_index("col")
    ap = c % GR
    cg = c // GR
    half = c // NROW
    part = c % NROW
    is_p = cg == r
    not_p = jnp.logical_not(is_p)

    barrier = pltpu.get_barrier_semaphore()

    def greet(i, n):
        pl.semaphore_signal(barrier, inc=1, device_id=(r, lax.rem(c + i, NCOL)), device_id_type=MESH)

        @pl.when(i < NROW)
        def _():
            pl.semaphore_signal(barrier, inc=1, device_id=(lax.rem(r + i, NROW), c), device_id_type=MESH)

        @pl.when(is_p)
        def _():
            other = lax.rem(c + i, NCOL)
            pl.semaphore_signal(barrier, inc=1, device_id=(other // GR, other), device_id_type=MESH)
        return n
    lax.fori_loop(1, NCOL, greet, 0)
    pl.semaphore_wait(barrier, NCOL - 1 + NROW - 1 + (NCOL - 1) * is_p.astype(jnp.int32))

    def rc(src, dst, ss, rs, dev):
        return pltpu.make_async_remote_copy(src_ref=src, dst_ref=dst, send_sem=ss, recv_sem=rs, device_id=dev,
                                            device_id_type=MESH)

    def each(lo, hi, fn):
        def body(i, n):
            fn(i)
            return n
        lax.fori_loop(lo, hi, body, 0)

    def g_copy(d):
        return rc(dchunk, diag.at[c], g_send.at[d], g_recv.at[d], (r, lax.rem(c + d, NCOL)))

    def g_from(d):
        return rc(dchunk, diag.at[lax.rem(c - d + NCOL, NCOL)], g_send.at[d], g_recv.at[d], (r, lax.rem(c + d, NCOL)))

    def zr_copy(it, d):
        return rc(zsrc.at[it], zbuf.at[it, ap], zr_send.at[it, d], z_recv.at[it, ap], (r, lax.rem(c + d, NCOL)))

    def zc_copy(it, d):
        return rc(zsrc.at[it], zbuf.at[it, 2], zc_send.at[it, d], z_recv.at[it, 2], (lax.rem(r + d, NROW), c))

    def z_from(it, slot):
        return rc(zsrc.at[it], zbuf.at[it, slot], zr_send.at[it, 0], z_recv.at[it, slot], (lax.rem(r + 1, NROW), c))

    def s_copy(it, k, d):
        other = lax.rem(c + d, NCOL)
        return rc(ssrc.at[it, k], sbuf.at[it, k, c], s_send.at[it, k, d], s_recv.at[it, k, c], (other // GR, other))

    def s_from(it, k, i):
        return rc(ssrc.at[it, k], sbuf.at[it, k, i], s_send.at[it, k, 0], s_recv.at[it, k, i], (i // GR, i))

    def c_copy(it, a):
        return rc(csrc.at[it, a], cbuf.at[it, c], c_send.at[it, a], c_recv.at[it, c], (r, GR * r + a))

    def c_from(it, i):
        return rc(csrc.at[it, 0], cbuf.at[it, i], c_send.at[it, 0], c_recv.at[it, i], (r, i))

    def b_copy(it):
        return rc(bsrc.at[it], bbuf.at[it, r], b_send.at[it], b_recv.at[it, r], (cg, c))

    def b_from(it, i):
        return rc(bsrc.at[it], bbuf.at[it, i], b_send.at[it], b_recv.at[it, i], (i, c))

    def f_copy(d):
        return rc(fsrc, fbuf.at[ap], f_send.at[d], f_recv.at[ap], (r, lax.rem(c + d, NCOL)))

    def f_from(a):
        return rc(fsrc, fbuf.at[a], f_send.at[0], f_recv.at[a], (r, GR * r + a))

    def total(it, k):
        def wait(i):
            @pl.when(i != c)
            def _():
                s_from(it, k, i).wait_recv()
        each(0, NCOL, wait)
        sbuf[it, k, c] = ssrc[it, k]
        return jnp.sum(sbuf[it, k], axis=0)

    X, RES, D, IM, RZ = range(5)

    def exchange(it, k, value):
        ssrc[it, k] = jnp.zeros((8, 128), F32) + jnp.sum(value)
        each(1, NCOL, lambda d: s_copy(it, k, d).start())

    @pl.when(is_p)
    def _():
        state[X] = jnp.zeros((8, 128), F32)
        state[RES] = rhs[ap]

    def solve(it):
        res = state[RES]
        z = matvec(xinv, res)
        for _ in range(REFINE):
            z = z + matvec(xinv, res - matvec(pmat, z))
        zsrc[it] = z
        each(1, NCOL, lambda d: zr_copy(it, d).start())
        each(1, NROW, lambda d: zc_copy(it, d).start())
        exchange(it, 0, res * z)
        zbuf[it, ap] = z
        zbuf[it, 2] = z

    for it in range(ITERS):
        @pl.when(is_p)
        def _():
            solve(it)
        if it == 0:
            cp = pltpu.make_async_copy(dchunk, diag.at[c], g_loc)
            cp.start()
            each(1, NCOL, lambda d: g_copy(d).start())

        for slot in range(3):
            @pl.when(not_p if slot == 2 else c != GR * r + slot)
            def _():
                z_from(it, slot).wait_recv()

        zc = zbuf[it, 2]
        back = [jnp.zeros((1, hi - lo), F32) for lo, hi in map(lanes, range(LT))]
        for a in range(GR):
            acc[a] = -spread(tile[a], zc)
            zcol = columns(zbuf[it, a])
            for t in range(LT):
                lo, hi = lanes(t)
                back[t] = back[t] + jnp.sum(tile[a, :, lo:hi] * zcol[:BLK, :hi - lo], axis=0, keepdims=True)
        rows = pl.ds(pl.multiple_of(part * CH, 8), CH)
        acc[half, rows, :] += spread(dchunk[...], zbuf[it, half])
        back[LT - 1] = jnp.concatenate([back[LT - 1], jnp.zeros((1, 128 * LT - BLK), F32)], axis=1)
        bsrc[it] = jnp.concatenate(back + [jnp.zeros((8 - LT, 128), F32)], axis=0)

        @pl.when(not_p)
        def _():
            b_copy(it).start()
        for a in range(GR):
            csrc[it, a] = fold(acc[a])

            @pl.when(c != GR * r + a)
            def _():
                c_copy(it, a).start()

        @pl.when(is_p)
        def _():
            cbuf[it, c] = csrc[it, ap]
            bbuf[it, r] = bsrc[it]

            def wait_c(i):
                @pl.when(i != c)
                def _():
                    c_from(it, i).wait_recv()

            def wait_b(i):
                @pl.when(i != r)
                def _():
                    b_from(it, i).wait_recv()
            rz = total(it, 0)
            each(0, NCOL, wait_c)
            each(0, NROW, wait_b)
            image = jnp.sum(cbuf[it], axis=0) - jnp.sum(bbuf[it], axis=0)
            direction = zsrc[it]
            if it > 0:
                beta = rz / state[RZ]
                direction = direction + beta * state[D]
                image = image + beta * state[IM]
            state[RZ] = rz
            state[D] = direction
            state[IM] = image
            exchange(it, 1, direction * image)
            alpha = rz / total(it, 1)
            state[X] = state[X] + alpha * direction
            state[RES] = state[RES] - alpha * image

    @pl.when(is_p)
    def _():
        fsrc[0] = state[X]
        fsrc[1] = state[RES]
        each(1, NCOL, lambda d: f_copy(d).start())
        fbuf[ap] = fsrc[...]

    for a in range(GR):
        @pl.when(c != GR * r + a)
        def _():
            f_from(a).wait_recv()
        sol[a] = fbuf[a, 0]
        resid[a] = fbuf[a, 1]

    pltpu.make_async_copy(dchunk, diag.at[c], g_loc).wait()
    each(1, NCOL, lambda d: g_from(d).wait_recv())
    each(1, NCOL, lambda d: g_copy(d).wait_send())
    for it in range(ITERS):
        @pl.when(not_p)
        def _():
            b_copy(it).wait_send()
        for a in range(GR):
            @pl.when(c != GR * r + a)
            def _():
                c_copy(it, a).wait_send()

    @pl.when(is_p)
    def _():
        for it in range(ITERS):
            each(1, NCOL, lambda d: zr_copy(it, d).wait_send())
            each(1, NROW, lambda d: zc_copy(it, d).wait_send())
            for k in range(2):
                each(1, NCOL, lambda d: s_copy(it, k, d).wait_send())
        each(1, NCOL, lambda d: f_copy(d).wait_send())


def gradients(tile, dchunk, xinv, pmat, rhs):
    vm = pl.BlockSpec(memory_space=pltpu.VMEM)
    dma = pltpu.SemaphoreType.DMA
    v = lambda *lead: pltpu.VMEM((*lead, 8, 128), F32)
    vec = jax.ShapeDtypeStruct((GR, 8, 128), F32)
    return pl.pallas_call(
        cg_kernel,
        out_shape=(jax.ShapeDtypeStruct((NCOL, CH, BLK), F32), vec, vec),
        in_specs=[vm] * 5,
        out_specs=(pl.BlockSpec(memory_space=pl.ANY), vm, vm),
        scratch_shapes=[
            v(ITERS, 3), v(ITERS), v(ITERS, NCOL), v(ITERS, GR), v(ITERS, NROW), v(ITERS), v(ITERS, 2, NCOL), v(ITERS, 2),
            v(GR, 2), v(2), pltpu.VMEM((GR, BLK, 128), F32), v(5),
            dma, dma((NCOL,)), dma((NCOL,)), dma((ITERS, NCOL)), dma((ITERS, NROW)), dma((ITERS, 3)),
            dma((ITERS, GR)), dma((ITERS,)), dma((ITERS, NCOL)), dma((ITERS, NROW)),
            dma((ITERS, 2, NCOL)), dma((ITERS, 2, NCOL)), dma((NCOL,)), dma((GR,)),
        ],
        compiler_params=pltpu.CompilerParams(collective_id=1, has_side_effects=True, vmem_limit_bytes=40 * 2**20),
        name="gradients",
    )(tile, dchunk, xinv, pmat, rhs)


def body(jac_row, jac_col, point_inv, pair_counts, camera_blocks, right_side):
    tile, dchunk, pg = form(minv_table(point_inv, pair_counts), stack_rows(jac_row), stack_rows(jac_col),
                            camera_blocks.reshape(NCOL, CH, BLK))
    xinv, pmat = inverse(pg.reshape(BLK, BLK), tile)
    wide = 128 * LT
    rhs = jnp.pad(right_side, ((0, 0), (0, wide - BLK))).reshape(GR, LT, 128)
    rhs = jnp.pad(rhs, ((0, 0), (0, 8 - LT), (0, 0)))
    diag, sol, res = gradients(tile, dchunk, xinv, pmat, rhs)
    back = lambda v: v[:, :LT].reshape(GR, wide)[:, :BLK]
    return tile[:, None], diag.reshape(GR, BLK, BLK), back(sol), back(res)


def solution(mesh):
    return jax.shard_map(
        body,
        mesh=mesh,
        in_specs=(
            P("row", "col", None, None, None, None, None),
            P("row", "col", None, None, None, None, None),
            P("row", "col", None, None, None, None),
            P("row", "col", None, None),
            P("row", None, None),
            P("row", None),
        ),
        out_specs=(
            P("row", "col", None, None),
            P("row", None, None),
            P("row", None),
            P("row", None),
        ),
        check_vma=False,
    )
```

time: 1170 us -> 447 us (0.38)
  Pallas kernels: 0 us -> 436 us
  other arithmetic: 365 us -> 1.7 us
  blocking collectives: 307 us -> 0 us
  waiting for transfers between devices: 226 us -> 0 us
  local copies, waits for them, and re-layouts: 141 us -> 7.47 us
  matrix products: 100 us -> 0 us
  between operations: 19.1 us -> 0.71 us
    pallas_call x0 -> x3, Pallas kernels: none -> 436 us  [the longest x1 339 us: form(): pl.pallas_call(form_kernel, out_shape=(jax.ShapeDtypeStruct((GR, BLK, BLK...]
    another operation x59 -> x0, other arithmetic: 326 us -> none  [the longest x21 203 us: body(): factor = jnp.linalg.cholesky(diagonal - pair_sum)]
    psum x5 -> x0, blocking collectives: 170 us -> none  [the longest x2 128 us: body(): summed = lax.psum(spread, ('row', 'col'))]
    psum x2 -> x0, waiting for transfers between devices: 166 us -> none  [the longest x1 110 us: body(): own_sum, pair_sum = lax.psum((own_terms, pair_terms), 'col')]
    all_to_all x2 -> x0, blocking collectives: 111 us -> none  [the longest x1 95.2 us: body(): lax.all_to_all(w_col, 'col', split_axis=0, concat_axis=2, tiled=True)]
    all_to_all x1 -> x0, waiting for transfers between devices: 59.9 us -> none  [body(): lax.all_to_all(w_row, 'col', split_axis=0, concat_axis=2, tiled=True)]
    another operation x44 -> x0, matrix products: 59 us -> none  [the longest x18 22 us: solve_blocks(): lax.linalg.triangular_solve(factor, vec[..., None], left_side=True, lower...]
    unnamed x58 -> x12, local copies, waits for them, and re-layouts: 49.5 us -> 5.95 us
  transfers between devices with their start and end apart: 3 -> 0, of which waited for: 3 -> 0; matrix products, arithmetic and copies ran while one was open for 6% -> 0% of each run, Pallas kernels for 0% -> 0%
where the time goes in v1:
time: 447 us; the launch traced here: 446 us
  Pallas kernels  436 us (98%)
  local copies, waits for them, and re-layouts  7.47 us (2%)
    pallas_call x1, Pallas kernels, form(): pl.pallas_call(form_kernel, out_shape=(jax.ShapeDtypeStruct((GR, BLK, BLK...  339 us
    pallas_call x1, Pallas kernels, gradients(): pl.pallas_call(cg_kernel, out_shape=(jax.ShapeDtypeStruct((NCOL, CH, BLK)...  92.2 us

profile of v1, /device:TPU:0, one launch (start us, length us, event | category | flops | bytes accessed | tf_op | source)
XLA Modules:
  0.0 446.3 jit_solution(2741355582014436285)
XLA Ops:
  0.6 0.7 pad.13
  1.3 0.8 fusion.1
  2.1 0.9 fusion
  3.0 0.1 reshape.55
  3.2 0.7 pad_bitcast_fusion.minv
  3.9 338.5 %form.1 = (f32[2,576,576]{2,1,0:T(8,128)}, f32[72,576]{1,0:T(8,128)}, f32[8,72,576]{2,1,0:T(8,128)}) custom-call(bf16[16,16,192]{2,1,0:T(8,128)(2,1)} %pad_bitcast_fusion.minv, bf16[16,384,576]{2,1,0:T(8,128)(2,1)} %bitcast.39, bf16[16,384,576]{2,1,0:T(8,128)(2,1)} %bitcast.40, f32[16,72,576]{2,1,0:T(8,128)} %bitcast.41), custom_call_target="tpu_custom_call" | custom-call | tf_op jit(solution)/shard_map/form/pallas_call | solution.py:212
  342.4 0.0 copy-start
  342.5 0.0 copy-start.1
  342.5 1.5 copy-done.1
  344.0 0.0 copy-start.2
  344.0 5.7 %inverse.1 = (f32[576,576]{1,0:T(8,128)S(1)}, f32[576,576]{1,0:T(8,128)S(1)}) custom-call(f32[576,576]{1,0:T(8,128)S(1)} %bitcast.38, f32[2,576,576]{2,1,0:T(8,128)} %get-tuple-element.12.tile), custom_call_target="tpu_custom_call" | custom-call | tf_op jit(solution)/shard_map/inverse/pallas_call | solution.py:317
  349.7 0.0 copy-done
  349.7 0.0 copy-done.2
  349.7 92.2 %gradients.1 = (f32[16,72,576]{2,1,0:T(8,128)S(1)}, f32[2,8,128]{2,1,0:T(8,128)S(1)}, f32[2,8,128]{2,1,0:T(8,128)S(1)}) custom-call(f32[2,576,576]{2,1,0:T(8,128)S(1)} %copy-done, f32[72,576]{1,0:T(8,128)S(1)} %copy-done.2, f32[576,576]{1,0:T(8,128)S(1)} %get-tuple-element.15.xinv, f32[576,576]{1,0:T(8,128)S(1)} %get-tuple-element.16.pmat, ...), custom_call_target="tpu_custom_call" | custom-call | tf_op jit(solution)/shard_map/gradients/pallas_call | solution.py:588
  441.9 0.6 copy.24
  442.5 0.6 copy.25
  443.1 1.6 copy.28
  444.7 1.6 copy.29
  (4 shorter events, 0.1 us)
Async XLA Ops:
  342.4 7.2 %copy-start = (f32[2,576,576]{2,1,0:T(8,128)S(1)}, f32[2,576,576]{2,1,0:T(8,128)}, u32[]{:S(2)}) copy-start(f32[2,576,576]{2,1,0:T(8,128)} %get-tuple-element.12.tile) | copy-start | bytes 7962628
  342.5 1.5 copy-start.1
  344.0 5.7 %copy-start.2 = (f32[72,576]{1,0:T(8,128)S(1)}, f32[72,576]{1,0:T(8,128)}, u32[]{:S(2)}) copy-start(f32[72,576]{1,0:T(8,128)} %get-tuple-element.13.dchunk) | copy-start | bytes 497668

commit v2 on v1

v2 whole, which is shorter than its diff:
```python
import jax
import jax.numpy as jnp
from jax import lax
from jax.experimental import pallas as pl
from jax.experimental.pallas import tpu as pltpu
from jax.sharding import PartitionSpec as P

MESH = pl.DeviceIdType.MESH
F32 = jnp.float32
BF16 = jnp.bfloat16
NROW, NCOL, GR, SLOT, BLK = 8, 16, 2, 64, 576
SIDE = 4
K3 = 3 * SLOT
CH = 72
WIDE = 640
CUT = 256
REST = BLK - CUT
ITERS = 2

OFF = (2, 1, 3, 0)
ORDER = [(u, v) for t in range(SIDE) for u in range(SIDE) for v in range(SIDE) if min(u, v) == t]


def pick(table, n):
    return sum(jnp.where(n == i, value, 0) for i, value in enumerate(table))


def tn(lhs, rhs):
    return lax.dot_general(lhs, rhs, (((0,), (0,)), ((), ())), preferred_element_type=F32)


def each(lo, hi, fn):
    def body(i, n):
        fn(i)
        return n
    lax.fori_loop(lo, hi, body, 0)


def remote(src, dst, ss, rs, dev):
    return pltpu.make_async_remote_copy(src_ref=src, dst_ref=dst, send_sem=ss, recv_sem=rs, device_id=dev,
                                        device_id_type=MESH)


def form_kernel(minv, wrow, wcol, cam, tile, dchunk, terms, pg_out,
                lrow, lcol, limg, rrow, rimg, big, ta_s, tb_s, ta_r, tb_r, p_s, p_r, h0_r, h1_r, srow, qrow, pg, camv, tsum,
                l_sem, cam_sem, w_send, w_recv, i_send, i_recv, t_send, t_recv, p_send, p_recv, h_send, h_recv,
                rs_send, rs_recv, pg_send, pg_recv):
    r = lax.axis_index("row")
    c = lax.axis_index("col")
    z, x = c // SIDE, lax.rem(c, SIDE)
    cg = c // GR
    g = GR * r + c // NROW
    part = c % NROW

    barrier = pltpu.get_barrier_semaphore()

    def greet(i):
        pl.semaphore_signal(barrier, inc=1, device_id=(r, lax.rem(c + i, NCOL)), device_id_type=MESH)

        @pl.when(i < NROW)
        def _():
            pl.semaphore_signal(barrier, inc=1, device_id=(lax.rem(r + i, NROW), c), device_id_type=MESH)
    each(1, NCOL, greet)

    def at(dz, dx):
        return lax.rem(z + dz, SIDE) * SIDE + lax.rem(x + dx, SIDE)

    def place(n):
        u1, v1 = pick([o[0] for o in ORDER], n), pick([o[1] for o in ORDER], n)
        return u1, v1, pick([OFF[o[0]] for o in ORDER], n), pick([OFF[o[1]] for o in ORDER], n)

    def loads(n):
        _, _, u, v = place(n)
        slot = lax.rem(n, 2)
        return [pltpu.make_async_copy(src.at[at(u, v)], dst.at[slot], l_sem.at[k, slot])
                for k, (src, dst) in enumerate(((wrow, lrow), (wcol, lcol)))]

    def sends(n, a):
        u1, v1, u, v = place(n)
        d, t = (u, v1) if a == 0 else (v, u1)
        dev = (r, at(u, 0) if a == 0 else at(0, v))
        k = jnp.maximum(d - 1, 0)
        rows = pl.ds(K3 * k, K3)
        return d > 0, [
            remote(wrow.at[at(u, v), pl.ds(K3 * a, K3)], rrow.at[a, t, rows], w_send.at[a, n], w_recv.at[a, t, k], dev),
            remote(limg.at[n, a], rimg.at[a, t, rows], i_send.at[a, n], i_recv.at[a, t, k], dev)]

    def term(n):
        _, _, u, v = place(n)
        j = at(u, v)
        dev = (j // GR, c)
        s = lax.rem(j, GR)
        return j, [remote(ta_s.at[n], ta_r.at[r, s], t_send.at[0, n], t_recv.at[0, r, s], dev),
                   remote(tb_s.at[n], tb_r.at[r, s], t_send.at[1, n], t_recv.at[1, r, s], dev)]

    cam_copy = pltpu.make_async_copy(cam.at[c], camv, cam_sem)
    cam_copy.start()
    for cp in loads(0):
        cp.start()
    tile[...] = jnp.zeros_like(tile)
    row_i = lax.broadcasted_iota(jnp.int32, (SLOT, K3), 0)
    col_i = lax.broadcasted_iota(jnp.int32, (SLOT, K3), 1)
    eye = jnp.where(lax.rem(col_i, SLOT) == row_i, 1.0, 0.0).astype(F32)
    pl.semaphore_wait(barrier, NCOL - 1 + NROW - 1)

    def local(n):
        _, _, u, v = place(n)
        slot = lax.rem(n, 2)

        @pl.when(n + 1 < NCOL)
        def _():
            for cp in loads(n + 1):
                cp.start()
        for a in range(GR):
            goes, cps = sends(n, a)

            @pl.when(goes)
            def _():
                cps[0].start()
        for cp in loads(n):
            cp.wait()
        j = at(u, v)
        top, bot = [], []
        for a in range(GR):
            ent = minv[j, 8 * a:8 * a + 8, :].astype(F32)
            for k in range(3):
                big[a, SLOT * k:SLOT * (k + 1), :] = (eye * ent[k:k + 1, :]).astype(BF16)
            wr = lrow[slot, K3 * a:K3 * (a + 1), :]
            wc = lcol[slot, K3 * a:K3 * (a + 1), :]
            limg[n, a] = jnp.dot(big[a], wc, preferred_element_type=F32).astype(BF16)
            goes, cps = sends(n, a)

            @pl.when(goes)
            def _():
                cps[1].start()
            ri = jnp.dot(big[a], wr, preferred_element_type=F32).astype(BF16)
            tile[a, CUT:, :] += tn(wr[:, CUT:], ri)
            tile[a, :CUT, :CUT] += tn(wr[:, :CUT], ri[:, :CUT])
        wc0, wc1 = lcol[slot, :K3, :], lcol[slot, K3:, :]
        ta_s[n] = (tn(wc0[:, CUT:], limg[n, 0]) + tn(wc1[:, CUT:], limg[n, 1])).astype(BF16)
        tb_s[n] = (tn(wc0[:, :CUT], limg[n, 0, :, :CUT]) + tn(wc1[:, :CUT], limg[n, 1, :, :CUT])).astype(BF16)
        _, cps = term(n)

        @pl.when(j // GR != r)
        def _():
            for cp in cps:
                cp.start()

        @pl.when(j // GR == r)
        def _():
            s = lax.rem(j, GR)
            ta_r[r, s] = ta_s[n]
            tb_r[r, s] = tb_s[n]
    each(0, NCOL, local)

    def along(a, off):
        return (r, at(0, off) if a == 0 else at(off, 0))

    def own_rows(a, t):
        j = at(0, OFF[t]) if a == 0 else at(OFF[t], 0)
        return pltpu.make_async_copy(wrow.at[j, pl.ds(K3 * a, K3)], lrow.at[a, pl.ds(0, K3)], l_sem.at[0, a])

    def arrive(a, t):
        for k in range(SIDE - 1):
            rows = pl.ds(K3 * k, K3)
            dev = (r, at(k + 1, 0))
            remote(wrow.at[0, pl.ds(0, K3)], rrow.at[a, t, rows], w_send.at[a, 0], w_recv.at[a, t, k], dev).wait_recv()
            remote(limg.at[0, a], rimg.at[a, t, rows], i_send.at[a, 0], i_recv.at[a, t, k], dev).wait_recv()

    def partial(a, t, lo, hi):
        own = ORDER.index((SIDE - 1, t) if a == 0 else (t, SIDE - 1))
        return tn(rrow[a, t, :, lo:hi], rimg[a, t]) + tn(lrow[a, :K3, lo:hi], limg[own, a])

    blocks = ((0, 256), (256, 512), (512, 576))

    def relays(a):
        return [remote(p_s.at[a, 0, pl.ds(0, CUT)], h0_r.at[a], h_send.at[a, 0], h_recv.at[a, 0], along(a, 1)),
                remote(p_s.at[a, 0, pl.ds(CUT, REST)], h1_r.at[a], h_send.at[a, 1], h_recv.at[a, 1], along(a, 3))]

    def p_copy(a, t):
        return remote(p_s.at[a, t], p_r.at[a, t - 1], p_send.at[a, t - 1], p_recv.at[a, t - 1], along(a, OFF[t]))

    def pairs(t):
        for a in range(GR):
            own_rows(a, t).start()
        for a in range(GR):
            own_rows(a, t).wait()
            arrive(a, t)
            if t > 0:
                relays(a)[t - 1].wait_recv()
            for lo, hi in blocks:
                out = partial(a, t, lo, hi)
                if t == 1 and hi <= CUT:
                    out = out + h0_r[a, lo:hi, :].astype(F32)
                if t == 2 and lo >= CUT:
                    out = out + h1_r[a, lo - CUT:hi - CUT, :].astype(F32)
                p_s[a, t, lo:hi, :] = out.astype(BF16)
            for cp in relays(a) if t == 0 else [p_copy(a, t)]:
                cp.start()
    for t in range(SIDE - 1):
        pairs(t)

    def term_sum(i):
        for s in range(GR):
            @pl.when(i != r)
            def _():
                remote(ta_s.at[0], ta_r.at[i, s], t_send.at[0, 0], t_recv.at[0, i, s], (i, c)).wait_recv()
                remote(tb_s.at[0], tb_r.at[i, s], t_send.at[1, 0], t_recv.at[1, i, s], (i, c)).wait_recv()
            tile[s, CUT:, :] += ta_r[i, s].astype(F32)
            tile[s, :CUT, :CUT] += tb_r[i, s].astype(F32)
    each(0, NROW, term_sum)
    for a in range(GR):
        tile[a, :CUT, CUT:] = tile[a, CUT:, :CUT].T
    for m in range(NCOL):
        a, i = divmod(m, NROW)
        srow[m] = tile[a, CH * i:CH * (i + 1), :].astype(BF16)

    def row_copy(d):
        j = lax.rem(c + d, NCOL)
        return remote(srow.at[j], qrow.at[d], rs_send.at[d], rs_recv.at[d], (r, j))
    each(1, NCOL, lambda d: row_copy(d).start())

    last = SIDE - 1
    for a in range(GR):
        own_rows(a, last).start()
    for a in range(GR):
        own_rows(a, last).wait()
        arrive(a, last)
        for lo, hi in blocks:
            tile[a, lo:hi, :] = partial(a, last, lo, hi)

    tsum[...] = srow[c].astype(F32)

    def row_sum(d):
        row_copy(d).wait_recv()
        tsum[...] += qrow[d].astype(F32)
    each(1, NCOL, row_sum)
    cam_copy.wait()
    total = tsum[...]
    short = total.astype(BF16)
    on = (lax.broadcasted_iota(jnp.int32, (CH, BLK), 0) + part * CH) == lax.broadcasted_iota(jnp.int32, (CH, BLK), 1)
    rest = jnp.sum(jnp.where(on, total - short.astype(F32), 0.0), axis=1, keepdims=True).astype(BF16).astype(F32)
    terms[:, :BLK] = short
    terms[:, BLK:] = jnp.broadcast_to(rest, (CH, WIDE - BLK)).astype(BF16)
    dchunk[...] = camv[...] - (short.astype(F32) + jnp.where(on, rest, 0.0))

    is_p = cg == r

    def pg_copy(i):
        return remote(dchunk, pg.at[i], pg_send, pg_recv.at[i], (r, g))

    @pl.when(g != c)
    def _():
        pg_copy(part).start()

    for t in (1, 2):
        for a in range(GR):
            p_copy(a, t).wait_recv()
            tile[a] += p_r[a, t - 1].astype(F32)

    def gather(i):
        src_c = (c % GR) * NROW + i

        @pl.when(jnp.logical_and(is_p, src_c != c))
        def _():
            pg_copy(i).wait_recv()
            pg_out[i] = pg[i]

        @pl.when(jnp.logical_and(is_p, src_c == c))
        def _():
            pg_out[i] = dchunk[...]

        @pl.when(jnp.logical_not(is_p))
        def _():
            rows = lax.broadcasted_iota(jnp.int32, (CH, BLK), 0) + i * CH
            cols = lax.broadcasted_iota(jnp.int32, (CH, BLK), 1)
            pg_out[i] = jnp.where(rows == cols, 1.0, 0.0).astype(F32)
    each(0, NROW, gather)

    @pl.when(g != c)
    def _():
        pg_copy(part).wait_send()

    def drain(n):
        for a in range(GR):
            goes, cps = sends(n, a)

            @pl.when(goes)
            def _():
                for cp in cps:
                    cp.wait_send()
        j, cps = term(n)

        @pl.when(j // GR != r)
        def _():
            for cp in cps:
                cp.wait_send()

        @pl.when(n > 0)
        def _():
            row_copy(n).wait_send()
    each(0, NCOL, drain)
    for a in range(GR):
        for cp in relays(a) + [p_copy(a, 1), p_copy(a, 2)]:
            cp.wait_send()


def form(minv, wrow, wcol, cam):
    any_ = pl.BlockSpec(memory_space=pl.ANY)
    vm = pl.BlockSpec(memory_space=pltpu.VMEM)
    dma = pltpu.SemaphoreType.DMA
    legs = SIDE - 1
    return pl.pallas_call(
        form_kernel,
        out_shape=(jax.ShapeDtypeStruct((GR, BLK, BLK), F32), jax.ShapeDtypeStruct((CH, BLK), F32),
                   jax.ShapeDtypeStruct((CH, WIDE), BF16), jax.ShapeDtypeStruct((NROW, CH, BLK), F32)),
        in_specs=[vm] + [any_] * 3,
        out_specs=(vm, vm, vm, vm),
        scratch_shapes=[
            pltpu.VMEM((2, GR * K3, BLK), BF16),
            pltpu.VMEM((2, GR * K3, BLK), BF16),
            pltpu.VMEM((NCOL, GR, K3, BLK), BF16),
            pltpu.VMEM((GR, SIDE, legs * K3, BLK), BF16),
            pltpu.VMEM((GR, SIDE, legs * K3, BLK), BF16),
            pltpu.VMEM((GR, K3, K3), BF16),
            pltpu.VMEM((NCOL, REST, BLK), BF16),
            pltpu.VMEM((NCOL, CUT, CUT), BF16),
            pltpu.VMEM((NROW, GR, REST, BLK), BF16),
            pltpu.VMEM((NROW, GR, CUT, CUT), BF16),
            pltpu.VMEM((GR, legs, BLK, BLK), BF16),
            pltpu.VMEM((GR, 2, BLK, BLK), BF16),
            pltpu.VMEM((GR, CUT, BLK), BF16),
            pltpu.VMEM((GR, REST, BLK), BF16),
            pltpu.VMEM((NCOL, CH, BLK), BF16),
            pltpu.VMEM((NCOL, CH, BLK), BF16),
            pltpu.VMEM((NROW, CH, BLK), F32),
            pltpu.VMEM((CH, BLK), F32),
            pltpu.VMEM((CH, BLK), F32),
            dma((2, 2)), dma, dma((GR, NCOL)), dma((GR, SIDE, legs)), dma((GR, NCOL)), dma((GR, SIDE, legs)),
            dma((2, NCOL)), dma((2, NROW, GR)), dma((GR, 2)), dma((GR, 2)), dma((GR, 2)), dma((GR, 2)),
            dma((NCOL,)), dma((NCOL,)), dma, dma((NROW,)),
        ],
        compiler_params=pltpu.CompilerParams(collective_id=0, has_side_effects=True, vmem_limit_bytes=62 * 2**20),
        name="form",
    )(minv, wrow, wcol, cam)


def minv_table(point_inv, pair_counts):
    inv = point_inv.reshape(NCOL, GR, SLOT, 3, 3)
    live = lax.broadcasted_iota(jnp.int32, (NCOL, GR, SLOT), 2) < pair_counts.reshape(NCOL, GR)[:, :, None]
    masked = inv * live[..., None, None].astype(BF16)
    rows = jnp.transpose(masked, (0, 1, 3, 4, 2)).reshape(NCOL, GR, 3, K3)
    return jnp.pad(rows, ((0, 0), (0, 0), (0, 5), (0, 0))).reshape(NCOL, 16, K3)


def stack_rows(jac):
    return jnp.transpose(jac.reshape(jac.shape[2:]), (0, 1, 3, 2, 4)).reshape(NCOL, GR * K3, BLK)


def mm(lhs, rhs):
    return jnp.dot(lhs.astype(BF16), rhs.astype(BF16), preferred_element_type=F32)


def mm_high(lhs, rhs):
    return jnp.dot(lhs, rhs, preferred_element_type=F32, precision=lax.Precision.HIGHEST)


def inverse_kernel(pg, tile, xinv, pmat, tile_out, both, e, y, res, sem, out_sem):
    r = lax.axis_index("row")
    c = lax.axis_index("col")
    is_p = (c // GR == r).astype(F32)
    cp = pltpu.make_async_copy(tile, both, sem)
    keep = pltpu.make_async_copy(both, tile_out, out_sem)
    cp.start()
    rows = lax.broadcasted_iota(jnp.int32, (BLK, BLK), 0)
    cols = lax.broadcasted_iota(jnp.int32, (BLK, BLK), 1)
    eye = jnp.where(rows == cols, 1.0, 0.0).astype(F32)
    cp.wait()
    keep.start()
    wide = 0.5 * pg[...] - both[c % GR] * is_p
    p = wide + wide.T
    pmat[...] = p
    dd = p * eye
    s_row = lax.rsqrt(jnp.sum(dd, axis=0, keepdims=True))
    s_col = lax.rsqrt(jnp.sum(dd, axis=1, keepdims=True))
    b = p * s_row * s_col
    e[...] = eye - b
    e2 = mm(e[...], e[...])
    f2 = jnp.sum(e2 * e2)

    @pl.when(f2 < 0.9)
    def _():
        y[...] = e[...] + e2 + mm(e[...], e2)

    @pl.when(jnp.logical_not(f2 < 0.9))
    def _():
        big = jnp.max(jnp.sum(jnp.abs(eye - e[...]), axis=1, keepdims=True))
        y[...] = eye * (1.0 / big - 1.0)

    def residual(mul):
        out = e[...] - y[...] + mul(y[...], e[...])
        res[...] = out
        return jnp.sum(out * out)

    def more(state):
        step, size = state
        return jnp.logical_and(size > 1.6e-5, step < 64)

    def newton(state):
        step, _ = state

        def low():
            y[...] = y[...] + res[...] + mm(res[...], y[...])
            return residual(mm)

        def high():
            y[...] = y[...] + res[...] + mm_high(res[...], y[...])
            return residual(mm_high)
        return step + 1, lax.cond(step < 6, low, high)
    lax.while_loop(more, newton, (jnp.int32(0), residual(mm)))
    xinv[...] = (eye + y[...]) * s_row * s_col
    keep.wait()


def inverse(pg, tile):
    vm = pl.BlockSpec(memory_space=pltpu.VMEM)
    sq = jax.ShapeDtypeStruct((BLK, BLK), F32)
    return pl.pallas_call(
        inverse_kernel,
        out_shape=(sq, sq, jax.ShapeDtypeStruct((GR, BLK, BLK), F32)),
        in_specs=[vm, pl.BlockSpec(memory_space=pl.ANY)],
        out_specs=(vm, vm, pl.BlockSpec(memory_space=pl.ANY)),
        scratch_shapes=[pltpu.VMEM((GR, BLK, BLK), F32)] + [pltpu.VMEM((BLK, BLK), F32)] * 3 + [pltpu.SemaphoreType.DMA] * 2,
        compiler_params=pltpu.CompilerParams(vmem_limit_bytes=48 * 2**20),
        name="inverse",
    )(pg, tile)


LT = 5
REFINE = 2


def lanes(t):
    return 128 * t, min(128 * (t + 1), BLK)


def spread(mat, vec):
    rows = mat.shape[0]
    acc = jnp.zeros((rows, 128), F32)
    for t in range(LT):
        lo, hi = lanes(t)
        part = mat[:, lo:hi] * vec[t:t + 1, :hi - lo]
        if hi - lo < 128:
            part = jnp.concatenate([part, jnp.zeros((rows, 128 - (hi - lo)), F32)], axis=1)
        acc = acc + part
    return acc


def fold(acc):
    out = []
    for t in range(LT):
        lo, hi = lanes(t)
        blk = acc[lo:hi, :]
        if hi - lo < 128:
            blk = jnp.concatenate([blk, jnp.zeros((128 - (hi - lo), 128), F32)], axis=0)
        out.append(jnp.sum(blk.T, axis=0, keepdims=True))
    return jnp.concatenate(out + [jnp.zeros((8 - LT, 128), F32)], axis=0)


def columns(vec):
    return jnp.concatenate([jnp.broadcast_to(vec[t:t + 1, :], (128, 128)).T for t in range(LT)], axis=0)


def matvec(mat, vec):
    return fold(spread(mat, vec))


def cg_kernel(tile, dchunk, xinv, pmat, rhs, sol, resid,
              zbuf, zsrc, cbuf, csrc, bbuf, bsrc, sbuf, ssrc, fbuf, fsrc, acc, state,
              zr_send, zc_send, z_recv, c_send, b_send, c_recv, b_recv,
              s_send, s_recv, f_send, f_recv):
    r = lax.axis_index("row")
    c = lax.axis_index("col")
    ap = c % GR
    cg = c // GR
    half = c // NROW
    part = c % NROW
    is_p = cg == r
    not_p = jnp.logical_not(is_p)

    barrier = pltpu.get_barrier_semaphore()

    def greet(i, n):
        pl.semaphore_signal(barrier, inc=1, device_id=(r, lax.rem(c + i, NCOL)), device_id_type=MESH)

        @pl.when(i < NROW)
        def _():
            pl.semaphore_signal(barrier, inc=1, device_id=(lax.rem(r + i, NROW), c), device_id_type=MESH)

        @pl.when(is_p)
        def _():
            other = lax.rem(c + i, NCOL)
            pl.semaphore_signal(barrier, inc=1, device_id=(other // GR, other), device_id_type=MESH)
        return n
    lax.fori_loop(1, NCOL, greet, 0)
    pl.semaphore_wait(barrier, NCOL - 1 + NROW - 1 + (NCOL - 1) * is_p.astype(jnp.int32))

    def zr_copy(it, d):
        return remote(zsrc.at[it], zbuf.at[it, ap], zr_send.at[it, d], z_recv.at[it, ap], (r, lax.rem(c + d, NCOL)))

    def zc_copy(it, d):
        return remote(zsrc.at[it], zbuf.at[it, 2], zc_send.at[it, d], z_recv.at[it, 2], (lax.rem(r + d, NROW), c))

    def z_from(it, slot):
        return remote(zsrc.at[it], zbuf.at[it, slot], zr_send.at[it, 0], z_recv.at[it, slot], (lax.rem(r + 1, NROW), c))

    def s_copy(k, d):
        other = lax.rem(c + d, NCOL)
        return remote(ssrc.at[k], sbuf.at[k, c], s_send.at[k, d], s_recv.at[k], (other // GR, other))

    def c_copy(it, a):
        return remote(csrc.at[it, a], cbuf.at[it, c], c_send.at[it, a], c_recv.at[it], (r, GR * r + a))

    def b_copy(it):
        return remote(bsrc.at[it], bbuf.at[it, r], b_send.at[it], b_recv.at[it], (cg, c))

    def take(buf, sem, count):
        pltpu.make_async_copy(buf.at[pl.ds(0, count)], buf.at[pl.ds(0, count)], sem).wait()

    def f_copy(d):
        return remote(fsrc, fbuf.at[ap], f_send.at[d], f_recv.at[ap], (r, lax.rem(c + d, NCOL)))

    def f_from(a):
        return remote(fsrc, fbuf.at[a], f_send.at[0], f_recv.at[a], (r, GR * r + a))

    def exchange(k, top, bottom):
        upper = lax.broadcasted_iota(jnp.int32, (8, 128), 0) < 4
        ssrc[k] = jnp.where(upper, jnp.sum(top), jnp.sum(bottom))
        each(1, NCOL, lambda d: s_copy(k, d).start())

    def totals(k):
        take(sbuf.at[k], s_recv.at[k], NCOL - 1)
        sbuf[k, c] = ssrc[k]
        both = jnp.sum(sbuf[k], axis=0)
        return both[0:1, :], both[4:5, :]

    def apply(vec):
        out = matvec(xinv, vec)
        for _ in range(REFINE):
            out = out + matvec(xinv, vec - matvec(pmat, out))
        return out

    def spread_out(it, vec):
        zsrc[it] = vec
        each(1, NCOL, lambda d: zr_copy(it, d).start())
        each(1, NROW, lambda d: zc_copy(it, d).start())
        zbuf[it, ap] = vec
        zbuf[it, 2] = vec

    def products(it):
        for slot in range(3):
            @pl.when(not_p if slot == 2 else c != GR * r + slot)
            def _():
                z_from(it, slot).wait_recv()

        zc = zbuf[it, 2]
        back = [jnp.zeros((1, hi - lo), F32) for lo, hi in map(lanes, range(LT))]
        for a in range(GR):
            acc[a] = -spread(tile[a], zc)
            zcol = columns(zbuf[it, a])
            for t in range(LT):
                lo, hi = lanes(t)
                back[t] = back[t] + jnp.sum(tile[a, :, lo:hi] * zcol[:BLK, :hi - lo], axis=0, keepdims=True)
        rows = pl.ds(pl.multiple_of(part * CH, 8), CH)
        acc[half, rows, :] += spread(dchunk[...], zbuf[it, half])
        back[LT - 1] = jnp.concatenate([back[LT - 1], jnp.zeros((1, 128 * LT - BLK), F32)], axis=1)
        bsrc[it] = jnp.concatenate(back + [jnp.zeros((8 - LT, 128), F32)], axis=0)

        @pl.when(not_p)
        def _():
            b_copy(it).start()
        for a in range(GR):
            csrc[it, a] = fold(acc[a])

            @pl.when(c != GR * r + a)
            def _():
                c_copy(it, a).start()

    def collect(it):
        take(cbuf.at[it], c_recv.at[it], NCOL - 1)
        take(bbuf.at[it], b_recv.at[it], NROW - 1)
        cbuf[it, c] = csrc[it, ap]
        bbuf[it, r] = bsrc[it]
        return jnp.sum(cbuf[it], axis=0) - jnp.sum(bbuf[it], axis=0)

    @pl.when(is_p)
    def _():
        spread_out(0, apply(rhs[ap]))
    products(0)

    @pl.when(is_p)
    def _():
        image = collect(0)
        state[0] = image
        spread_out(1, apply(image))
        exchange(0, rhs[ap] * zsrc[0], zsrc[0] * image)
    products(1)

    @pl.when(is_p)
    def _():
        first, image = zsrc[0], state[0]
        rz, curve = totals(0)
        alpha = rz / curve
        res = rhs[ap] - alpha * image
        second = first - alpha * zsrc[1]
        exchange(1, res * second, res * second)
        moved = image - alpha * collect(1)
        rz_next, _ = totals(1)
        beta = rz_next / rz
        direction = second + beta * first
        image = moved + beta * image
        exchange(2, direction * image, direction * image)
        curve, _ = totals(2)
        step = rz_next / curve
        fsrc[0] = alpha * first + step * direction
        fsrc[1] = res - step * image
        each(1, NCOL, lambda d: f_copy(d).start())
        fbuf[ap] = fsrc[...]

    for a in range(GR):
        @pl.when(c != GR * r + a)
        def _():
            f_from(a).wait_recv()
        sol[a] = fbuf[a, 0]
        resid[a] = fbuf[a, 1]

    for it in range(ITERS):
        @pl.when(not_p)
        def _():
            b_copy(it).wait_send()
        for a in range(GR):
            @pl.when(c != GR * r + a)
            def _():
                c_copy(it, a).wait_send()

    @pl.when(is_p)
    def _():
        for it in range(ITERS):
            each(1, NCOL, lambda d: zr_copy(it, d).wait_send())
            each(1, NROW, lambda d: zc_copy(it, d).wait_send())
        for k in range(3):
            each(1, NCOL, lambda d: s_copy(k, d).wait_send())
        each(1, NCOL, lambda d: f_copy(d).wait_send())


def gradients(tile, dchunk, xinv, pmat, rhs):
    vm = pl.BlockSpec(memory_space=pltpu.VMEM)
    dma = pltpu.SemaphoreType.DMA
    v = lambda *lead: pltpu.VMEM((*lead, 8, 128), F32)
    vec = jax.ShapeDtypeStruct((GR, 8, 128), F32)
    return pl.pallas_call(
        cg_kernel,
        out_shape=(vec, vec),
        in_specs=[vm] * 5,
        out_specs=(vm, vm),
        scratch_shapes=[
            v(ITERS, 3), v(ITERS), v(ITERS, NCOL), v(ITERS, GR), v(ITERS, NROW), v(ITERS), v(3, NCOL), v(3),
            v(GR, 2), v(2), pltpu.VMEM((GR, BLK, 128), F32), v(1),
            dma((ITERS, NCOL)), dma((ITERS, NROW)), dma((ITERS, 3)),
            dma((ITERS, GR)), dma((ITERS,)), dma((ITERS,)), dma((ITERS,)),
            dma((3, NCOL)), dma((3,)), dma((NCOL,)), dma((GR,)),
        ],
        compiler_params=pltpu.CompilerParams(collective_id=1, has_side_effects=True, vmem_limit_bytes=40 * 2**20),
        name="gradients",
    )(tile, dchunk, xinv, pmat, rhs)


def subtract_kernel(cam, terms, out):
    rows = lax.broadcasted_iota(jnp.int32, (CH, BLK), 0)
    cols = lax.broadcasted_iota(jnp.int32, (CH, BLK), 1)
    for a in range(GR):
        for lo in range(0, BLK, CH):
            part = terms[a, lo:lo + CH, :]
            rest = part[:, BLK:BLK + 1].astype(F32)
            out[a, lo:lo + CH, :] = cam[a, lo:lo + CH, :] - (
                part[:, :BLK].astype(F32) + jnp.where(rows + lo == cols, rest, 0.0))


def subtract(cam, terms):
    vm = pl.BlockSpec(memory_space=pltpu.VMEM)
    return pl.pallas_call(
        subtract_kernel,
        out_shape=jax.ShapeDtypeStruct((GR, BLK, BLK), F32),
        in_specs=[vm, vm],
        out_specs=vm,
        compiler_params=pltpu.CompilerParams(vmem_limit_bytes=24 * 2**20),
        name="subtract",
    )(cam, terms)


def body(jac_row, jac_col, point_inv, pair_counts, camera_blocks, right_side):
    tile, dchunk, terms, pg = form(minv_table(point_inv, pair_counts), stack_rows(jac_row), stack_rows(jac_col),
                                   camera_blocks.reshape(NCOL, CH, BLK))
    xinv, pmat, pairs = inverse(pg.reshape(BLK, BLK), tile)
    wide = 128 * LT
    rhs = jnp.pad(right_side, ((0, 0), (0, wide - BLK))).reshape(GR, LT, 128)
    rhs = jnp.pad(rhs, ((0, 0), (0, 8 - LT), (0, 0)))
    diag = subtract(camera_blocks, lax.all_gather(terms, "col", axis=0, tiled=True).reshape(GR, BLK, WIDE))
    sol, res = gradients(tile, dchunk, xinv, pmat, rhs)
    back = lambda v: v[:, :LT].reshape(GR, wide)[:, :BLK]
    return pairs[:, None], diag, back(sol), back(res)


def solution(mesh):
    return jax.shard_map(
        body,
        mesh=mesh,
        in_specs=(
            P("row", "col", None, None, None, None, None),
            P("row", "col", None, None, None, None, None),
            P("row", "col", None, None, None, None),
            P("row", "col", None, None),
            P("row", None, None),
            P("row", None),
        ),
        out_specs=(
            P("row", "col", None, None),
            P("row", None, None),
            P("row", None),
            P("row", None),
        ),
        check_vma=False,
    )
```

time: 447 us -> 235 us (0.53)
  Pallas kernels: 436 us -> 213 us
  between operations: 0.71 us -> 14.1 us
    pallas_call x1, Pallas kernels: 339 us -> 156 us  [form(): pl.pallas_call(form_kernel, out_shape=(jax.ShapeDtypeStruct((GR, BLK, BLK...]
    pallas_call x2 -> x3, Pallas kernels: 97.9 us -> 57.4 us  [the longest x1 47.4 us: gradients(): pl.pallas_call(cg_kernel, out_shape=(vec, vec), in_specs=[vm] * 5, out_sp...]
  transfers between devices with their start and end apart: 0 -> 1, of which waited for: 0 -> 0; matrix products, arithmetic and copies ran while one was open for 0% -> 1% of each run, Pallas kernels for 0% -> 24%
where the time goes in v2:
time: 235 us; the launch traced here: 234 us
  Pallas kernels  213 us (91%)
  between operations  14.1 us (6%)
  local copies, waits for them, and re-layouts  4.97 us (2%)
    pallas_call x1, Pallas kernels, form(): pl.pallas_call(form_kernel, out_shape=(jax.ShapeDtypeStruct((GR, BLK, BLK...  156 us
    pallas_call x1, Pallas kernels, gradients(): pl.pallas_call(cg_kernel, out_shape=(vec, vec), in_specs=[vm] * 5, out_sp...  47.4 us
    pallas_call x1, Pallas kernels, inverse(): pl.pallas_call(inverse_kernel, out_shape=(sq, sq, jax.ShapeDtypeStruct((G...  8.13 us
  transfers between devices with their start and end apart: 1, of which 0 were waited for; matrix products, arithmetic and copies ran while one was open for 1% of the time, Pallas kernels for 24%

profile of v2, /device:TPU:0, one launch (start us, length us, event | category | flops | bytes accessed | tf_op | source)
XLA Modules:
  0.0 234.3 jit_solution(6699089755180596535)
XLA Ops:
  7.2 0.0 all-gather.2.cloned.1.call-start
  7.2 0.8 fusion.1
  8.0 0.9 fusion
  8.9 0.1 reshape.55
  9.1 0.7 pad_bitcast_fusion.minv
  9.8 0.0 copy-start.5
  9.8 156.0 %form.1 = (f32[2,576,576]{2,1,0:T(8,128)}, f32[72,576]{1,0:T(8,128)}, bf16[72,640]{1,0:T(8,128)(2,1)}, f32[8,72,576]{2,1,0:T(8,128)}) custom-call(bf16[16,16,192]{2,1,0:T(8,128)(2,1)} %pad_bitcast_fusion.minv, bf16[16,384,576]{2,1,0:T(8,128)(2,1)} %bitcast.39, bf16[16,384,576]{2,1,0:T(8,128)(2,1)} %bitcast.40, f32[16,72,576]{2,1,0:T(8,128)} %bitcast.36), custom_call_target="tpu_custom_call" | custom-call | tf_op jit(solution)/shard_map/form/pallas_call | solution.py:313
  165.7 0.0 all-gather.2.cloned.1.call-update
  165.8 0.0 copy-done.5
  165.8 0.0 copy-start.1
  165.8 0.0 copy-start.3
  165.8 1.5 copy-done.3
  167.4 0.0 copy-start.4
  167.4 8.1 %inverse.1 = (f32[576,576]{1,0:T(8,128)S(1)}, f32[576,576]{1,0:T(8,128)S(1)}, f32[2,576,576]{2,1,0:T(8,128)}) custom-call(f32[576,576]{1,0:T(8,128)S(1)} %bitcast.38, f32[2,576,576]{2,1,0:T(8,128)} %get-tuple-element.14.tile), custom_call_target="tpu_custom_call" | custom-call | tf_op jit(solution)/shard_map/inverse/pallas_call | solution.py:428
  175.5 0.0 copy-done.1
  175.5 0.0 copy-done.4
  175.5 0.0 copy-start
  175.5 47.4 %gradients.1 = (f32[2,8,128]{2,1,0:T(8,128)S(1)}, f32[2,8,128]{2,1,0:T(8,128)S(1)}) custom-call(f32[2,576,576]{2,1,0:T(8,128)S(1)} %copy-done.1, f32[72,576]{1,0:T(8,128)S(1)} %copy-done.4, f32[576,576]{1,0:T(8,128)S(1)} %get-tuple-element.18.xinv, f32[576,576]{1,0:T(8,128)S(1)} %get-tuple-element.19.pmat, f32[2,8,128]{2,1,0:T(8,128)S(1)} %pad.14.rhs), custom_call_target="tpu_custom_call" | custom-call | tf_op jit(solution)/shard_map/gradients/pallas_call | solution.py:661
  222.9 0.6 copy.25
  223.5 0.6 copy.24
  224.1 0.0 all-gather.2.cloned.1.call-done
  224.1 0.0 copy-done
  224.1 1.4 copy-done.2
  225.5 1.9 subtract.1
  (6 shorter events, 0.1 us)
Async XLA Ops:
  7.2 217.0 %all-gather.2.cloned.1.call-start = ((), (), s32[]{:S(2)}) async-start(), calls=%async_computation | async-start | bytes 1566720 | tf_op jit(solution)/shard_map/all_gather | solution.py:708
  9.8 156.0 %copy-start.5 = (f32[2,576]{1,0:T(2,128)S(1)}, f32[2,576]{1,0:T(2,128)}, u32[]{:S(2)}) copy-start(f32[2,576]{1,0:T(2,128)} %param.11) | copy-start | bytes 13828
  165.8 9.7 %copy-start.1 = (f32[2,576,576]{2,1,0:T(8,128)S(1)}, f32[2,576,576]{2,1,0:T(8,128)}, u32[]{:S(2)}) copy-start(f32[2,576,576]{2,1,0:T(8,128)} %get-tuple-element.14.tile) | copy-start | bytes 7962628
  165.8 1.5 copy-start.3
  167.4 8.2 %copy-start.4 = (f32[72,576]{1,0:T(8,128)S(1)}, f32[72,576]{1,0:T(8,128)}, u32[]{:S(2)}) copy-start(f32[72,576]{1,0:T(8,128)} %get-tuple-element.17.dchunk) | copy-start | bytes 497668
  175.5 48.6 %copy-start = (f32[2,576,576]{2,1,0:T(8,128)S(1)}, f32[2,576,576]{2,1,0:T(8,128)}, u32[]{:S(2)}) copy-start(f32[2,576,576]{2,1,0:T(8,128)} %cam.1) | copy-start | bytes 7962628
  224.1 1.4 copy-start.2
Sparse Core Ops, SparseCore 0:
  165.9 49.6 all-gather.1

commit v3 on v2

--- a/solution.py
+++ b/solution.py
@@ -13,6 +13,7 @@
 K3 = 3 * SLOT
 CH = 72
 WIDE = 640
+MAIN = 512
 CUT = 256
 REST = BLK - CUT
 ITERS = 2
@@ -42,7 +43,7 @@
 
 
 def form_kernel(minv, wrow, wcol, cam, tile, dchunk, terms, pg_out,
-                lrow, lcol, limg, rrow, rimg, big, ta_s, tb_s, ta_r, tb_r, p_s, p_r, h0_r, h1_r, srow, qrow, pg, camv, tsum,
+                lrow, lcol, limg, rrow, rimg, big, ta_s, tb_s, ta_r, tb_r, p_s, p_r, h0_r, h1_r, srow, qrow, pg, camv, tsum, dsend,
                 l_sem, cam_sem, w_send, w_recv, i_send, i_recv, t_send, t_recv, p_send, p_recv, h_send, h_recv,
                 rs_send, rs_recv, pg_send, pg_recv):
     r = lax.axis_index("row")
@@ -82,7 +83,7 @@
         k = jnp.maximum(d - 1, 0)
         rows = pl.ds(K3 * k, K3)
         return d > 0, [
-            remote(wrow.at[at(u, v), pl.ds(K3 * a, K3)], rrow.at[a, t, rows], w_send.at[a, n], w_recv.at[a, t, k], dev),
+            remote(wrow.at[at(u, v), pl.ds(K3 * a, K3), pl.ds(0, MAIN)], rrow.at[a, t, rows], w_send.at[a, n], w_recv.at[a, t, k], dev),
             remote(limg.at[n, a], rimg.at[a, t, rows], i_send.at[a, n], i_recv.at[a, t, k], dev)]
 
     def term(n):
@@ -98,6 +99,11 @@
     for cp in loads(0):
         cp.start()
     tile[...] = jnp.zeros_like(tile)
+    for ref in (ta_s, srow):
+        ref[:, :, MAIN:] = jnp.zeros((*ref.shape[:2], WIDE - MAIN), BF16)
+    for a in range(GR):
+        p_s[a, :, :, MAIN:] = jnp.zeros((SIDE - 1, BLK, WIDE - MAIN), BF16)
+    dsend[:, MAIN:] = jnp.zeros((CH, WIDE - MAIN), F32)
     row_i = lax.broadcasted_iota(jnp.int32, (SLOT, K3), 0)
     col_i = lax.broadcasted_iota(jnp.int32, (SLOT, K3), 1)
     eye = jnp.where(lax.rem(col_i, SLOT) == row_i, 1.0, 0.0).astype(F32)
@@ -127,7 +133,9 @@
                 big[a, SLOT * k:SLOT * (k + 1), :] = (eye * ent[k:k + 1, :]).astype(BF16)
             wr = lrow[slot, K3 * a:K3 * (a + 1), :]
             wc = lcol[slot, K3 * a:K3 * (a + 1), :]
-            limg[n, a] = jnp.dot(big[a], wc, preferred_element_type=F32).astype(BF16)
+            ci = jnp.dot(big[a], wc, preferred_element_type=F32)
+            limg[n, a, :, :MAIN] = ci[:, :MAIN].astype(BF16)
+            limg[n, a, :, MAIN:] = jnp.concatenate([ci[:, MAIN:], wr[:, MAIN:].astype(F32)], axis=1).astype(BF16)
             goes, cps = sends(n, a)
 
             @pl.when(goes)
@@ -137,7 +145,7 @@
             tile[a, CUT:, :] += tn(wr[:, CUT:], ri)
             tile[a, :CUT, :CUT] += tn(wr[:, :CUT], ri[:, :CUT])
         wc0, wc1 = lcol[slot, :K3, :], lcol[slot, K3:, :]
-        ta_s[n] = (tn(wc0[:, CUT:], limg[n, 0]) + tn(wc1[:, CUT:], limg[n, 1])).astype(BF16)
+        ta_s[n, :, :BLK] = (tn(wc0[:, CUT:], limg[n, 0, :, :BLK]) + tn(wc1[:, CUT:], limg[n, 1, :, :BLK])).astype(BF16)
         tb_s[n] = (tn(wc0[:, :CUT], limg[n, 0, :, :CUT]) + tn(wc1[:, :CUT], limg[n, 1, :, :CUT])).astype(BF16)
         _, cps = term(n)
 
@@ -164,12 +172,15 @@
         for k in range(SIDE - 1):
             rows = pl.ds(K3 * k, K3)
             dev = (r, at(k + 1, 0))
-            remote(wrow.at[0, pl.ds(0, K3)], rrow.at[a, t, rows], w_send.at[a, 0], w_recv.at[a, t, k], dev).wait_recv()
+            remote(wrow.at[0, pl.ds(0, K3), pl.ds(0, MAIN)], rrow.at[a, t, rows], w_send.at[a, 0], w_recv.at[a, t, k], dev).wait_recv()
             remote(limg.at[0, a], rimg.at[a, t, rows], i_send.at[a, 0], i_recv.at[a, t, k], dev).wait_recv()
 
     def partial(a, t, lo, hi):
         own = ORDER.index((SIDE - 1, t) if a == 0 else (t, SIDE - 1))
-        return tn(rrow[a, t, :, lo:hi], rimg[a, t]) + tn(lrow[a, :K3, lo:hi], limg[own, a])
+        own = tn(lrow[a, :K3, lo:hi], limg[own, a, :, :BLK])
+        if lo < MAIN:
+            return own + tn(rrow[a, t, :, lo:hi], rimg[a, t, :, :BLK])
+        return own + tn(rimg[a, t, :, lo:], rimg[a, t, :, :BLK])[hi - lo:, :]
 
     blocks = ((0, 256), (256, 512), (512, 576))
 
@@ -191,10 +202,10 @@
             for lo, hi in blocks:
                 out = partial(a, t, lo, hi)
                 if t == 1 and hi <= CUT:
-                    out = out + h0_r[a, lo:hi, :].astype(F32)
+                    out = out + h0_r[a, lo:hi, :BLK].astype(F32)
                 if t == 2 and lo >= CUT:
-                    out = out + h1_r[a, lo - CUT:hi - CUT, :].astype(F32)
-                p_s[a, t, lo:hi, :] = out.astype(BF16)
+                    out = out + h1_r[a, lo - CUT:hi - CUT, :BLK].astype(F32)
+                p_s[a, t, lo:hi, :BLK] = out.astype(BF16)
             for cp in relays(a) if t == 0 else [p_copy(a, t)]:
                 cp.start()
     for t in range(SIDE - 1):
@@ -206,14 +217,14 @@
             def _():
                 remote(ta_s.at[0], ta_r.at[i, s], t_send.at[0, 0], t_recv.at[0, i, s], (i, c)).wait_recv()
                 remote(tb_s.at[0], tb_r.at[i, s], t_send.at[1, 0], t_recv.at[1, i, s], (i, c)).wait_recv()
-            tile[s, CUT:, :] += ta_r[i, s].astype(F32)
+            tile[s, CUT:, :] += ta_r[i, s, :, :BLK].astype(F32)
             tile[s, :CUT, :CUT] += tb_r[i, s].astype(F32)
     each(0, NROW, term_sum)
     for a in range(GR):
         tile[a, :CUT, CUT:] = tile[a, CUT:, :CUT].T
     for m in range(NCOL):
         a, i = divmod(m, NROW)
-        srow[m] = tile[a, CH * i:CH * (i + 1), :].astype(BF16)
+        srow[m, :, :BLK] = tile[a, CH * i:CH * (i + 1), :].astype(BF16)
 
     def row_copy(d):
         j = lax.rem(c + d, NCOL)
@@ -229,11 +240,11 @@
         for lo, hi in blocks:
             tile[a, lo:hi, :] = partial(a, last, lo, hi)
 
-    tsum[...] = srow[c].astype(F32)
+    tsum[...] = srow[c, :, :BLK].astype(F32)
 
     def row_sum(d):
         row_copy(d).wait_recv()
-        tsum[...] += qrow[d].astype(F32)
+        tsum[...] += qrow[d, :, :BLK].astype(F32)
     each(1, NCOL, row_sum)
     cam_copy.wait()
     total = tsum[...]
@@ -244,10 +255,11 @@
     terms[:, BLK:] = jnp.broadcast_to(rest, (CH, WIDE - BLK)).astype(BF16)
     dchunk[...] = camv[...] - (short.astype(F32) + jnp.where(on, rest, 0.0))
 
+    dsend[:, :BLK] = dchunk[...]
     is_p = cg == r
 
     def pg_copy(i):
-        return remote(dchunk, pg.at[i], pg_send, pg_recv.at[i], (r, g))
+        return remote(dsend, pg.at[i], pg_send, pg_recv.at[i], (r, g))
 
     @pl.when(g != c)
     def _():
@@ -256,7 +268,7 @@
     for t in (1, 2):
         for a in range(GR):
             p_copy(a, t).wait_recv()
-            tile[a] += p_r[a, t - 1].astype(F32)
+            tile[a] += p_r[a, t - 1, :, :BLK].astype(F32)
 
     def gather(i):
         src_c = (c % GR) * NROW + i
@@ -264,7 +276,7 @@
         @pl.when(jnp.logical_and(is_p, src_c != c))
         def _():
             pg_copy(i).wait_recv()
-            pg_out[i] = pg[i]
+            pg_out[i] = pg[i, :, :BLK]
 
         @pl.when(jnp.logical_and(is_p, src_c == c))
         def _():
@@ -319,23 +331,24 @@
         scratch_shapes=[
             pltpu.VMEM((2, GR * K3, BLK), BF16),
             pltpu.VMEM((2, GR * K3, BLK), BF16),
-            pltpu.VMEM((NCOL, GR, K3, BLK), BF16),
-            pltpu.VMEM((GR, SIDE, legs * K3, BLK), BF16),
-            pltpu.VMEM((GR, SIDE, legs * K3, BLK), BF16),
+            pltpu.VMEM((NCOL, GR, K3, WIDE), BF16),
+            pltpu.VMEM((GR, SIDE, legs * K3, MAIN), BF16),
+            pltpu.VMEM((GR, SIDE, legs * K3, WIDE), BF16),
             pltpu.VMEM((GR, K3, K3), BF16),
-            pltpu.VMEM((NCOL, REST, BLK), BF16),
+            pltpu.VMEM((NCOL, REST, WIDE), BF16),
             pltpu.VMEM((NCOL, CUT, CUT), BF16),
-            pltpu.VMEM((NROW, GR, REST, BLK), BF16),
+            pltpu.VMEM((NROW, GR, REST, WIDE), BF16),
             pltpu.VMEM((NROW, GR, CUT, CUT), BF16),
-            pltpu.VMEM((GR, legs, BLK, BLK), BF16),
-            pltpu.VMEM((GR, 2, BLK, BLK), BF16),
-            pltpu.VMEM((GR, CUT, BLK), BF16),
-            pltpu.VMEM((GR, REST, BLK), BF16),
-            pltpu.VMEM((NCOL, CH, BLK), BF16),
-            pltpu.VMEM((NCOL, CH, BLK), BF16),
-            pltpu.VMEM((NROW, CH, BLK), F32),
+            pltpu.VMEM((GR, legs, BLK, WIDE), BF16),
+            pltpu.VMEM((GR, 2, BLK, WIDE), BF16),
+            pltpu.VMEM((GR, CUT, WIDE), BF16),
+            pltpu.VMEM((GR, REST, WIDE), BF16),
+            pltpu.VMEM((NCOL, CH, WIDE), BF16),
+            pltpu.VMEM((NCOL, CH, WIDE), BF16),
+            pltpu.VMEM((NROW, CH, WIDE), F32),
             pltpu.VMEM((CH, BLK), F32),
             pltpu.VMEM((CH, BLK), F32),
+            pltpu.VMEM((CH, WIDE), F32),
             dma((2, 2)), dma, dma((GR, NCOL)), dma((GR, SIDE, legs)), dma((GR, NCOL)), dma((GR, SIDE, legs)),
             dma((2, NCOL)), dma((2, NROW, GR)), dma((GR, 2)), dma((GR, 2)), dma((GR, 2)), dma((GR, 2)),
             dma((NCOL,)), dma((NCOL,)), dma, dma((NROW,)),

time: 235 us -> 227 us (0.966)
  Pallas kernels: 213 us -> 205 us
    pallas_call x1, Pallas kernels: 156 us -> 148 us  [form(): pl.pallas_call(form_kernel, out_shape=(jax.ShapeDtypeStruct((GR, BLK, BLK...]
where the time goes in v3:
time: 227 us; the launch traced here: 226 us
  Pallas kernels  205 us (90%)
  between operations  14.1 us (6%)
  local copies, waits for them, and re-layouts  4.97 us (2%)
    pallas_call x1, Pallas kernels, form(): pl.pallas_call(form_kernel, out_shape=(jax.ShapeDtypeStruct((GR, BLK, BLK...  148 us
    pallas_call x1, Pallas kernels, gradients(): pl.pallas_call(cg_kernel, out_shape=(vec, vec), in_specs=[vm] * 5, out_sp...  49 us
    pallas_call x1, Pallas kernels, inverse(): pl.pallas_call(inverse_kernel, out_shape=(sq, sq, jax.ShapeDtypeStruct((G...  6.17 us
  transfers between devices with their start and end apart: 1, of which 0 were waited for; matrix products, arithmetic and copies ran while one was open for 1% of the time, Pallas kernels for 24%

profile of v3, /device:TPU:0, one launch (start us, length us, event | category | flops | bytes accessed | tf_op | source)
XLA Modules:
  0.0 225.7 jit_solution(9852305392557612620)
XLA Ops:
  7.2 0.0 all-gather.2.cloned.1.call-start
  7.2 0.8 fusion.1
  8.0 0.9 fusion
  8.9 0.1 reshape.55
  9.1 0.7 pad_bitcast_fusion.minv
  9.8 0.0 copy-start.5
  9.8 147.7 %form.1 = (f32[2,576,576]{2,1,0:T(8,128)}, f32[72,576]{1,0:T(8,128)}, bf16[72,640]{1,0:T(8,128)(2,1)}, f32[8,72,576]{2,1,0:T(8,128)}) custom-call(bf16[16,16,192]{2,1,0:T(8,128)(2,1)} %pad_bitcast_fusion.minv, bf16[16,384,576]{2,1,0:T(8,128)(2,1)} %bitcast.39, bf16[16,384,576]{2,1,0:T(8,128)(2,1)} %bitcast.40, f32[16,72,576]{2,1,0:T(8,128)} %bitcast.36), custom_call_target="tpu_custom_call" | custom-call | tf_op jit(solution)/shard_map/form/pallas_call | solution.py:325
  157.5 0.0 all-gather.2.cloned.1.call-update
  157.5 0.0 copy-done.5
  157.5 0.0 copy-start.1
  157.6 0.0 copy-start.3
  157.6 1.5 copy-done.3
  159.1 0.0 copy-start.4
  159.1 6.2 %inverse.1 = (f32[576,576]{1,0:T(8,128)S(1)}, f32[576,576]{1,0:T(8,128)S(1)}, f32[2,576,576]{2,1,0:T(8,128)}) custom-call(f32[576,576]{1,0:T(8,128)S(1)} %bitcast.38, f32[2,576,576]{2,1,0:T(8,128)} %get-tuple-element.14.tile), custom_call_target="tpu_custom_call" | custom-call | tf_op jit(solution)/shard_map/inverse/pallas_call | solution.py:441
  165.3 0.0 copy-done.1
  165.3 0.0 copy-done.4
  165.3 0.0 copy-start
  165.3 49.0 %gradients.1 = (f32[2,8,128]{2,1,0:T(8,128)S(1)}, f32[2,8,128]{2,1,0:T(8,128)S(1)}) custom-call(f32[2,576,576]{2,1,0:T(8,128)S(1)} %copy-done.1, f32[72,576]{1,0:T(8,128)S(1)} %copy-done.4, f32[576,576]{1,0:T(8,128)S(1)} %get-tuple-element.18.xinv, f32[576,576]{1,0:T(8,128)S(1)} %get-tuple-element.19.pmat, f32[2,8,128]{2,1,0:T(8,128)S(1)} %pad.14.rhs), custom_call_target="tpu_custom_call" | custom-call | tf_op jit(solution)/shard_map/gradients/pallas_call | solution.py:674
  214.3 0.6 copy.25
  214.9 0.6 copy.24
  215.5 0.0 all-gather.2.cloned.1.call-done
  215.5 0.0 copy-done
  215.5 1.4 copy-done.2
  216.9 1.9 subtract.1
  (6 shorter events, 0.1 us)
Async XLA Ops:
  7.2 208.3 %all-gather.2.cloned.1.call-start = ((), (), s32[]{:S(2)}) async-start(), calls=%async_computation | async-start | bytes 1566720 | tf_op jit(solution)/shard_map/all_gather | solution.py:721
  9.8 147.8 %copy-start.5 = (f32[2,576]{1,0:T(2,128)S(1)}, f32[2,576]{1,0:T(2,128)}, u32[]{:S(2)}) copy-start(f32[2,576]{1,0:T(2,128)} %param.11) | copy-start | bytes 13828
  157.5 7.7 %copy-start.1 = (f32[2,576,576]{2,1,0:T(8,128)S(1)}, f32[2,576,576]{2,1,0:T(8,128)}, u32[]{:S(2)}) copy-start(f32[2,576,576]{2,1,0:T(8,128)} %get-tuple-element.14.tile) | copy-start | bytes 7962628
  157.6 1.5 copy-start.3
  159.1 6.2 %copy-start.4 = (f32[72,576]{1,0:T(8,128)S(1)}, f32[72,576]{1,0:T(8,128)}, u32[]{:S(2)}) copy-start(f32[72,576]{1,0:T(8,128)} %get-tuple-element.17.dchunk) | copy-start | bytes 497668
  165.3 50.2 %copy-start = (f32[2,576,576]{2,1,0:T(8,128)S(1)}, f32[2,576,576]{2,1,0:T(8,128)}, u32[]{:S(2)}) copy-start(f32[2,576,576]{2,1,0:T(8,128)} %cam.1) | copy-start | bytes 7962628
  215.5 1.4 copy-start.2
Sparse Core Ops, SparseCore 0:
  157.6 49.5 all-gather.1

commit v4 on v3

--- a/solution.py
+++ b/solution.py
@@ -444,7 +444,7 @@
         in_specs=[vm, pl.BlockSpec(memory_space=pl.ANY)],
         out_specs=(vm, vm, pl.BlockSpec(memory_space=pl.ANY)),
         scratch_shapes=[pltpu.VMEM((GR, BLK, BLK), F32)] + [pltpu.VMEM((BLK, BLK), F32)] * 3 + [pltpu.SemaphoreType.DMA] * 2,
-        compiler_params=pltpu.CompilerParams(vmem_limit_bytes=48 * 2**20),
+        compiler_params=pltpu.CompilerParams(vmem_limit_bytes=60 * 2**20),
         name="inverse",
     )(pg, tile)
 
@@ -488,9 +488,9 @@
     return fold(spread(mat, vec))
 
 
-def cg_kernel(tile, dchunk, xinv, pmat, rhs, sol, resid,
+def cg_kernel(tile_in, dchunk, xinv_in, pmat_in, rhs, terms, gathered, sol, resid, tile, xinv, pmat,
               zbuf, zsrc, cbuf, csrc, bbuf, bsrc, sbuf, ssrc, fbuf, fsrc, acc, state,
-              zr_send, zc_send, z_recv, c_send, b_send, c_recv, b_recv,
+              m_sem, g_loc, g_send, g_recv, zr_send, zc_send, z_recv, c_send, b_send, c_recv, b_recv,
               s_send, s_recv, f_send, f_recv):
     r = lax.axis_index("row")
     c = lax.axis_index("col")
@@ -500,6 +500,10 @@
     part = c % NROW
     is_p = cg == r
     not_p = jnp.logical_not(is_p)
+    held = [pltpu.make_async_copy(src, dst, m_sem.at[n])
+            for n, (src, dst) in enumerate(((tile_in, tile), (xinv_in, xinv), (pmat_in, pmat)))]
+    for cp in held:
+        cp.start()
 
     barrier = pltpu.get_barrier_semaphore()
 
@@ -517,6 +521,32 @@
         return n
     lax.fori_loop(1, NCOL, greet, 0)
     pl.semaphore_wait(barrier, NCOL - 1 + NROW - 1 + (NCOL - 1) * is_p.astype(jnp.int32))
+    for cp in held:
+        cp.wait()
+
+    z, x = c // SIDE, lax.rem(c, SIDE)
+    four = pl.ds(SIDE * z, SIDE)
+
+    def g_copy(d):
+        return remote(terms, gathered.at[c], g_send.at[0, d], g_recv.at[0, d], (r, SIDE * z + lax.rem(x + d, SIDE)))
+
+    def g_from(d):
+        other = SIDE * z + lax.rem(x + SIDE - d, SIDE)
+        return remote(terms, gathered.at[other], g_send.at[0, d], g_recv.at[0, d], (r, other))
+
+    def g_second(d):
+        return remote(gathered.at[four], gathered.at[four], g_send.at[1, d], g_recv.at[1, d],
+                      (r, SIDE * lax.rem(z + d, SIDE) + x))
+
+    def g_last(d):
+        other = SIDE * lax.rem(z + SIDE - d, SIDE)
+        there = gathered.at[pl.ds(other, SIDE)]
+        return remote(there, there, g_send.at[1, d], g_recv.at[1, d], (r, other + x))
+
+    def pass_on():
+        g_own.wait()
+        each(1, SIDE, lambda d: g_from(d).wait_recv())
+        each(1, SIDE, lambda d: g_second(d).start())
 
     def zr_copy(it, d):
         return remote(zsrc.at[it], zbuf.at[it, ap], zr_send.at[it, d], z_recv.at[it, ap], (r, lax.rem(c + d, NCOL)))
@@ -609,7 +639,11 @@
     @pl.when(is_p)
     def _():
         spread_out(0, apply(rhs[ap]))
+    g_own = pltpu.make_async_copy(terms, gathered.at[c], g_loc)
+    g_own.start()
+    each(1, SIDE, lambda d: g_copy(d).start())
     products(0)
+    pl.when(is_p)(pass_on)
 
     @pl.when(is_p)
     def _():
@@ -618,6 +652,8 @@
         spread_out(1, apply(image))
         exchange(0, rhs[ap] * zsrc[0], zsrc[0] * image)
     products(1)
+
+    pl.when(not_p)(pass_on)
 
     @pl.when(is_p)
     def _():
@@ -646,6 +682,9 @@
             f_from(a).wait_recv()
         sol[a] = fbuf[a, 0]
         resid[a] = fbuf[a, 1]
+    each(1, SIDE, lambda d: g_last(d).wait_recv())
+    each(1, SIDE, lambda d: g_copy(d).wait_send())
+    each(1, SIDE, lambda d: g_second(d).wait_send())
 
     for it in range(ITERS):
         @pl.when(not_p)
@@ -666,26 +705,28 @@
         each(1, NCOL, lambda d: f_copy(d).wait_send())
 
 
-def gradients(tile, dchunk, xinv, pmat, rhs):
+def gradients(tile, dchunk, xinv, pmat, rhs, terms):
     vm = pl.BlockSpec(memory_space=pltpu.VMEM)
     dma = pltpu.SemaphoreType.DMA
     v = lambda *lead: pltpu.VMEM((*lead, 8, 128), F32)
     vec = jax.ShapeDtypeStruct((GR, 8, 128), F32)
+    any_ = pl.BlockSpec(memory_space=pl.ANY)
     return pl.pallas_call(
         cg_kernel,
-        out_shape=(vec, vec),
-        in_specs=[vm] * 5,
-        out_specs=(vm, vm),
+        out_shape=(jax.ShapeDtypeStruct((NCOL, CH, WIDE), BF16), vec, vec),
+        in_specs=[any_, vm, any_, any_, vm, vm],
+        out_specs=(any_, vm, vm),
         scratch_shapes=[
+            pltpu.VMEM((GR, BLK, BLK), F32), pltpu.VMEM((BLK, BLK), F32), pltpu.VMEM((BLK, BLK), F32),
             v(ITERS, 3), v(ITERS), v(ITERS, NCOL), v(ITERS, GR), v(ITERS, NROW), v(ITERS), v(3, NCOL), v(3),
             v(GR, 2), v(2), pltpu.VMEM((GR, BLK, 128), F32), v(1),
-            dma((ITERS, NCOL)), dma((ITERS, NROW)), dma((ITERS, 3)),
+            dma((3,)), dma, dma((2, SIDE)), dma((2, SIDE)), dma((ITERS, NCOL)), dma((ITERS, NROW)), dma((ITERS, 3)),
             dma((ITERS, GR)), dma((ITERS,)), dma((ITERS,)), dma((ITERS,)),
             dma((3, NCOL)), dma((3,)), dma((NCOL,)), dma((GR,)),
         ],
-        compiler_params=pltpu.CompilerParams(collective_id=1, has_side_effects=True, vmem_limit_bytes=40 * 2**20),
+        compiler_params=pltpu.CompilerParams(collective_id=1, has_side_effects=True, vmem_limit_bytes=60 * 2**20),
         name="gradients",
-    )(tile, dchunk, xinv, pmat, rhs)
+    )(tile, dchunk, xinv, pmat, rhs, terms)
 
 
 def subtract_kernel(cam, terms, out):
@@ -718,8 +759,8 @@
     wide = 128 * LT
     rhs = jnp.pad(right_side, ((0, 0), (0, wide - BLK))).reshape(GR, LT, 128)
     rhs = jnp.pad(rhs, ((0, 0), (0, 8 - LT), (0, 0)))
-    diag = subtract(camera_blocks, lax.all_gather(terms, "col", axis=0, tiled=True).reshape(GR, BLK, WIDE))
-    sol, res = gradients(tile, dchunk, xinv, pmat, rhs)
+    gathered, sol, res = gradients(tile, dchunk, xinv, pmat, rhs, terms)
+    diag = subtract(camera_blocks, gathered.reshape(GR, BLK, WIDE))
     back = lambda v: v[:, :LT].reshape(GR, wide)[:, :BLK]
     return pairs[:, None], diag, back(sol), back(res)
 

time: 227 us -> 220 us (0.969)
  between operations: 14.1 us -> 0.71 us
  Pallas kernels: 205 us -> 212 us
    pallas_call x1, Pallas kernels: 49 us -> 53.2 us  [gradients(): pl.pallas_call(cg_kernel, out_shape=(jax.ShapeDtypeStruct((NCOL, CH, WIDE...]
    pallas_call x1, Pallas kernels: 6.17 us -> 9.1 us  [inverse(): pl.pallas_call(inverse_kernel, out_shape=(sq, sq, jax.ShapeDtypeStruct((G...]
  transfers between devices with their start and end apart: 1 -> 0, of which waited for: 0 -> 0; matrix products, arithmetic and copies ran while one was open for 1% -> 0% of each run, Pallas kernels for 24% -> 0%
where the time goes in v4:
time: 220 us; the launch traced here: 218 us
  Pallas kernels  212 us (96%)
  local copies, waits for them, and re-layouts  4.03 us (2%)
    pallas_call x1, Pallas kernels, form(): pl.pallas_call(form_kernel, out_shape=(jax.ShapeDtypeStruct((GR, BLK, BLK...  148 us
    pallas_call x1, Pallas kernels, gradients(): pl.pallas_call(cg_kernel, out_shape=(jax.ShapeDtypeStruct((NCOL, CH, WIDE...  53.2 us
    pallas_call x1, Pallas kernels, inverse(): pl.pallas_call(inverse_kernel, out_shape=(sq, sq, jax.ShapeDtypeStruct((G...  9.1 us

profile of v4, /device:TPU:0, one launch (start us, length us, event | category | flops | bytes accessed | tf_op | source)
XLA Modules:
  0.0 218.3 jit_solution(9714097085189701742)
XLA Ops:
  0.6 0.8 fusion.1
  1.4 0.9 fusion
  2.3 0.1 reshape.55
  2.5 0.7 pad_bitcast_fusion.minv
  3.2 147.6 %form.1 = (f32[2,576,576]{2,1,0:T(8,128)}, f32[72,576]{1,0:T(8,128)}, bf16[72,640]{1,0:T(8,128)(2,1)}, f32[8,72,576]{2,1,0:T(8,128)}) custom-call(bf16[16,16,192]{2,1,0:T(8,128)(2,1)} %pad_bitcast_fusion.minv, bf16[16,384,576]{2,1,0:T(8,128)(2,1)} %bitcast.38, bf16[16,384,576]{2,1,0:T(8,128)(2,1)} %bitcast.39, f32[16,72,576]{2,1,0:T(8,128)} %bitcast.36), custom_call_target="tpu_custom_call" | custom-call | tf_op jit(solution)/shard_map/form/pallas_call | solution.py:325
  150.8 0.0 copy-start.4
  150.8 9.1 %inverse.1 = (f32[576,576]{1,0:T(8,128)}, f32[576,576]{1,0:T(8,128)}, f32[2,576,576]{2,1,0:T(8,128)}) custom-call(f32[576,576]{1,0:T(8,128)} %bitcast.40, f32[2,576,576]{2,1,0:T(8,128)} %get-tuple-element.15.tile.tile_in), custom_call_target="tpu_custom_call" | custom-call | tf_op jit(solution)/shard_map/inverse/pallas_call | solution.py:441
  159.9 0.0 copy-done.4
  160.0 0.6 pad.14.rhs
  160.6 0.0 copy-start
  160.6 53.2 %gradients.1 = (bf16[16,72,640]{2,1,0:T(8,128)(2,1)}, f32[2,8,128]{2,1,0:T(8,128)}, f32[2,8,128]{2,1,0:T(8,128)}) custom-call(f32[2,576,576]{2,1,0:T(8,128)} %get-tuple-element.15.tile.tile_in, f32[72,576]{1,0:T(8,128)} %get-tuple-element.17.dchunk, f32[576,576]{1,0:T(8,128)} %get-tuple-element.18.xinv_in, f32[576,576]{1,0:T(8,128)} %get-tuple-element.19.pmat_in, ...), custom_call_target="tpu_custom_call" | custom-call | tf_op jit(solution)/shard_map/gradients/pallas_call | solution.py:714
  213.8 0.0 copy-done
  213.8 0.0 copy-start.1
  213.8 1.4 copy-done.1
  215.2 0.0 copy-start.2
  215.2 0.0 copy-start.3
  215.2 1.9 subtract.1
  217.1 0.0 copy-done.2
  217.1 0.0 copy-done.3
  217.1 0.6 copy.25
  217.7 0.6 copy.24
  (4 shorter events, 0.1 us)
Async XLA Ops:
  150.8 9.1 %copy-start.4 = (f32[2,576]{1,0:T(2,128)S(1)}, f32[2,576]{1,0:T(2,128)}, u32[]{:S(2)}) copy-start(f32[2,576]{1,0:T(2,128)} %param.11) | copy-start | bytes 13828
  160.6 53.2 %copy-start = (f32[2,576,576]{2,1,0:T(8,128)S(1)}, f32[2,576,576]{2,1,0:T(8,128)}, u32[]{:S(2)}) copy-start(f32[2,576,576]{2,1,0:T(8,128)} %cam.1) | copy-start | bytes 7962628
  213.8 1.4 copy-start.1
  215.2 1.9 copy-start.2
  215.2 2.0 copy-start.3

commit v5 on v4

--- a/solution.py
+++ b/solution.py
@@ -217,9 +217,18 @@
             def _():
                 remote(ta_s.at[0], ta_r.at[i, s], t_send.at[0, 0], t_recv.at[0, i, s], (i, c)).wait_recv()
                 remote(tb_s.at[0], tb_r.at[i, s], t_send.at[1, 0], t_recv.at[1, i, s], (i, c)).wait_recv()
-            tile[s, CUT:, :] += ta_r[i, s, :, :BLK].astype(F32)
-            tile[s, :CUT, :CUT] += tb_r[i, s].astype(F32)
     each(0, NROW, term_sum)
+    for s in range(GR):
+        for lo in range(0, REST, SLOT):
+            out = tile[s, CUT + lo:CUT + lo + SLOT, :]
+            for i in range(NROW):
+                out = out + ta_r[i, s, lo:lo + SLOT, :BLK].astype(F32)
+            tile[s, CUT + lo:CUT + lo + SLOT, :] = out
+        for lo in range(0, CUT, SLOT):
+            out = tile[s, lo:lo + SLOT, :CUT]
+            for i in range(NROW):
+                out = out + tb_r[i, s, lo:lo + SLOT, :].astype(F32)
+            tile[s, lo:lo + SLOT, :CUT] = out
     for a in range(GR):
         tile[a, :CUT, CUT:] = tile[a, CUT:, :CUT].T
     for m in range(NCOL):

time: 220 us -> 218 us (level)
  no operation moved by 1% of the time
where the time goes in v5:
time: 218 us
  Pallas kernels  211 us (97%)
  local copies, waits for them, and re-layouts  4.03 us (2%)
    pallas_call x1, Pallas kernels, form(): pl.pallas_call(form_kernel, out_shape=(jax.ShapeDtypeStruct((GR, BLK, BLK...  148 us
    pallas_call x1, Pallas kernels, gradients(): pl.pallas_call(cg_kernel, out_shape=(jax.ShapeDtypeStruct((NCOL, CH, WIDE...  52.8 us
    pallas_call x1, Pallas kernels, inverse(): pl.pallas_call(inverse_kernel, out_shape=(sq, sq, jax.ShapeDtypeStruct((G...  9.1 us

profile of v5, /device:TPU:0, one launch (start us, length us, event | category | flops | bytes accessed | tf_op | source)
XLA Modules:
  0.0 217.8 jit_solution(14621345819862425870)
XLA Ops:
  0.6 0.8 fusion.1
  1.4 0.9 fusion
  2.3 0.1 reshape.55
  2.5 0.7 pad_bitcast_fusion.minv
  3.2 147.6 %form.1 = (f32[2,576,576]{2,1,0:T(8,128)}, f32[72,576]{1,0:T(8,128)}, bf16[72,640]{1,0:T(8,128)(2,1)}, f32[8,72,576]{2,1,0:T(8,128)}) custom-call(bf16[16,16,192]{2,1,0:T(8,128)(2,1)} %pad_bitcast_fusion.minv, bf16[16,384,576]{2,1,0:T(8,128)(2,1)} %bitcast.38, bf16[16,384,576]{2,1,0:T(8,128)(2,1)} %bitcast.39, f32[16,72,576]{2,1,0:T(8,128)} %bitcast.36), custom_call_target="tpu_custom_call" | custom-call | tf_op jit(solution)/shard_map/form/pallas_call | solution.py:334
  150.7 0.0 copy-start.4
  150.8 9.1 %inverse.1 = (f32[576,576]{1,0:T(8,128)}, f32[576,576]{1,0:T(8,128)}, f32[2,576,576]{2,1,0:T(8,128)}) custom-call(f32[576,576]{1,0:T(8,128)} %bitcast.40, f32[2,576,576]{2,1,0:T(8,128)} %get-tuple-element.15.tile.tile_in), custom_call_target="tpu_custom_call" | custom-call | tf_op jit(solution)/shard_map/inverse/pallas_call | solution.py:450
  159.9 0.0 copy-done.4
  159.9 0.6 pad.14.rhs
  160.5 0.0 copy-start
  160.5 52.8 %gradients.1 = (bf16[16,72,640]{2,1,0:T(8,128)(2,1)}, f32[2,8,128]{2,1,0:T(8,128)}, f32[2,8,128]{2,1,0:T(8,128)}) custom-call(f32[2,576,576]{2,1,0:T(8,128)} %get-tuple-element.15.tile.tile_in, f32[72,576]{1,0:T(8,128)} %get-tuple-element.17.dchunk, f32[576,576]{1,0:T(8,128)} %get-tuple-element.18.xinv_in, f32[576,576]{1,0:T(8,128)} %get-tuple-element.19.pmat_in, ...), custom_call_target="tpu_custom_call" | custom-call | tf_op jit(solution)/shard_map/gradients/pallas_call | solution.py:723
  213.3 0.0 copy-done
  213.3 0.0 copy-start.1
  213.3 1.4 copy-done.1
  214.7 0.0 copy-start.2
  214.7 0.0 copy-start.3
  214.7 1.9 subtract.1
  216.6 0.0 copy-done.2
  216.6 0.0 copy-done.3
  216.6 0.6 copy.25
  217.2 0.6 copy.24
  (4 shorter events, 0.1 us)
Async XLA Ops:
  150.7 9.1 %copy-start.4 = (f32[2,576]{1,0:T(2,128)S(1)}, f32[2,576]{1,0:T(2,128)}, u32[]{:S(2)}) copy-start(f32[2,576]{1,0:T(2,128)} %param.11) | copy-start | bytes 13828
  160.5 52.8 %copy-start = (f32[2,576,576]{2,1,0:T(8,128)S(1)}, f32[2,576,576]{2,1,0:T(8,128)}, u32[]{:S(2)}) copy-start(f32[2,576,576]{2,1,0:T(8,128)} %cam.1) | copy-start | bytes 7962628
  213.3 1.4 copy-start.1
  214.7 1.9 copy-start.2
  214.7 2.0 copy-start.3
